TPU v7x, 256 devices: a whole 4x4x8 slice. The times are simulated.
256 devices in a mesh: band: 2 (over core), patch: 128 (over z, x, y).
Axes of the slice: x: 4, y: 4, z: 8, core: 2. Of those that a mesh axis runs over, the one named last changes fastest.
Arguments:
- tiles: bfloat16 [2, 8192, 16384], P('band', 'patch'), may hold values from -6 to 6
- psf_coeff: bfloat16 [2, 8192, 5], P('band', 'patch'), may hold values from -4 to 4
- row_taps: bfloat16 [5, 41], replicated, may hold values from -1 to 1
- col_taps: bfloat16 [5, 41], replicated, may hold values from -1 to 1
- target_patch: int32 [2, 8192, 1], P('band', 'patch'), may hold values from 0 to 127; in each aligned block of 64 rows (0 to 63, 64 to 127, ..., all dimensions but the last counted through in order) at most 2 rows name the same one
- offsets: int32 [2, 8192, 2], P('band', 'patch'), may hold values from 0 to 125
- visits: int32 [2, 8192], P('band', 'patch'), may hold values from 1 to 9
- warp_rows: bfloat16 [2, 8192, 512], P('band', 'patch'), may hold values from 0.099609375 to 1
- warp_cols: bfloat16 [2, 8192, 512], P('band', 'patch'), may hold values from 0.099609375 to 1
- det_taps: float32 [9], replicated, may hold values from 0.05 to 0.4
- band_weight: float32 [2], P('band'), may hold values from 0.5 to 2
Outputs:
- coadd: float32 [2, 32768, 256], P('band', 'patch')
- detection: float32 [32768, 256], P('patch')
Inputs may be any that keep to these rules, and one draw needn't show every extreme that they name: `target_patch`: the tiles of one band held by one index of patch name any one patch at most 2 times, a bound that some block reaches.
All inputs are finite; a program needn't handle non-finite values.
Results may differ from a plain program's by a relative error of at most 0.0064.
Values may be sent and summed in bfloat16 or wider, within the bound.
A program may use at most 128 MiB of HBM per device.

v0:
```python
import math

import jax
import jax.numpy as jnp
from jax import lax
from jax.sharding import PartitionSpec as P

TILE = 128
BW = 4
PATCH = 256


def with_halo(cells, sides, width):
    for axis, dim in sides:
        count = lax.axis_size(axis)
        ends = count - 1
        head = lax.slice_in_dim(cells, 0, width, axis=dim)
        tail = lax.slice_in_dim(cells, cells.shape[dim] - width, cells.shape[dim], axis=dim)
        cells = jnp.concatenate(
            [
                lax.ppermute(tail, axis, [(i, (i + 1) % count) for i in range(ends)]),
                cells,
                lax.ppermute(head, axis, [((i + 1) % count, i) for i in range(ends)]),
            ],
            axis=dim,
        )
    return cells


def band_matrix(taps, edge):
    half_width = (taps.shape[-1] - 1) // 2
    row_index = lax.broadcasted_iota(jnp.int32, (edge, edge), 0)
    col_index = lax.broadcasted_iota(jnp.int32, (edge, edge), 1)
    offset = col_index - row_index + half_width
    inside = (offset >= 0) & (offset < taps.shape[-1])
    picked = jnp.take(taps, jnp.clip(offset, 0, taps.shape[-1] - 1), axis=-1)
    return jnp.where(inside, picked, jnp.zeros_like(picked))


def match_psf(images, coefficients, row_taps, col_taps):
    tile_edge = images.shape[-1]
    row_matrix = band_matrix(row_taps, tile_edge)
    col_matrix = band_matrix(col_taps, tile_edge)
    grouped = math.gcd(images.shape[0], 32)

    def one_group(paired):
        group_images, group_coeff = paired
        partial_value = jnp.einsum(
            "trc,kmc->trkm", group_images, col_matrix, preferred_element_type=jnp.float32
        )
        scaled = (partial_value * group_coeff.astype(jnp.float32)[:, None, :, None]).astype(
            jnp.bfloat16
        )
        return jnp.einsum(
            "kir,trkc->tic", row_matrix, scaled, preferred_element_type=jnp.float32
        ).astype(jnp.bfloat16)

    results = lax.map(
        one_group,
        (
            images.reshape(-1, grouped, tile_edge, tile_edge),
            coefficients.reshape(-1, grouped, coefficients.shape[-1]),
        ),
    )
    return results.reshape(images.shape)


def warp_block(totals, slot_items):
    numerator, coverage = totals
    matched, row_weights, col_weights, placing = slot_items
    slot_count = matched.shape[0]
    tile_edge = matched.shape[-1]
    patch_edge = numerator.shape[0]
    col_pos = lax.broadcasted_iota(jnp.int32, (slot_count, patch_edge, tile_edge), 1)
    col_src = lax.broadcasted_iota(jnp.int32, (slot_count, patch_edge, tile_edge), 2)
    col_gap = col_pos - col_src - placing[:, 1][:, None, None]
    row_pos = lax.broadcasted_iota(jnp.int32, (patch_edge, slot_count, tile_edge), 0)
    row_src = lax.broadcasted_iota(jnp.int32, (patch_edge, slot_count, tile_edge), 2)
    row_gap = row_pos - row_src - placing[:, 0][None, :, None]
    colmat = jnp.zeros((slot_count, patch_edge, tile_edge), jnp.float32)
    rowmat = jnp.zeros((patch_edge, slot_count, tile_edge), jnp.float32)
    for tap_index in range(row_weights.shape[1]):
        colmat = colmat + jnp.where(
            col_gap == tap_index, col_weights[:, tap_index, :][:, None, :].astype(jnp.float32), 0.0
        )
        rowmat = rowmat + jnp.where(
            row_gap == tap_index, row_weights[:, tap_index, :][None, :, :].astype(jnp.float32), 0.0
        )
    colmat = colmat.astype(jnp.bfloat16)
    rowmat = (rowmat * placing[:, 2].astype(jnp.float32)[None, :, None]).astype(jnp.bfloat16)
    shifted = jnp.einsum(
        "srj,sqj->srq", matched, colmat, preferred_element_type=jnp.float32
    ).astype(jnp.bfloat16)
    numerator = numerator + jnp.dot(
        rowmat.reshape(patch_edge, slot_count * tile_edge),
        shifted.reshape(slot_count * tile_edge, patch_edge),
        preferred_element_type=jnp.float32,
    )
    rowsum = jnp.sum(rowmat.astype(jnp.float32), axis=2)
    colsum = jnp.sum(colmat.astype(jnp.float32), axis=2)
    coverage = coverage + jnp.dot(rowsum, colsum, precision=lax.Precision.HIGHEST)
    return ((numerator, coverage), None)


def detect_sources(picture, det_taps):
    patch_edge = picture.shape[0]
    half_width = (det_taps.shape[0] - 1) // 2
    padded = with_halo(picture, (("patch", 0),), half_width)
    out_index = lax.broadcasted_iota(jnp.int32, (patch_edge, patch_edge + 2 * half_width), 0)
    pad_index = lax.broadcasted_iota(jnp.int32, (patch_edge, patch_edge + 2 * half_width), 1)
    row_gap = pad_index - out_index
    row_kernel = jnp.where(
        (row_gap >= 0) & (row_gap < det_taps.shape[0]),
        jnp.take(det_taps, jnp.clip(row_gap, 0, det_taps.shape[0] - 1)),
        0.0,
    )
    col_kernel = band_matrix(det_taps, patch_edge).T
    row_pass = jnp.dot(row_kernel, padded, precision=lax.Precision.HIGHEST)
    return jnp.dot(row_pass, col_kernel, precision=lax.Precision.HIGHEST)


def body(
    tiles,
    psf_coeff,
    row_taps,
    col_taps,
    target_patch,
    offsets,
    visits,
    warp_rows,
    warp_cols,
    det_taps,
    band_weight,
):
    patch_count = lax.axis_size("patch")
    flat_tiles = tiles[0]
    tile_count = flat_tiles.shape[0]
    capacity = max(2, 2 * tile_count // patch_count)
    slot_total = patch_count * capacity
    targets = target_patch[0, :, 0]
    row_order = lax.broadcasted_iota(jnp.int32, (tile_count, tile_count), 0)
    col_order = lax.broadcasted_iota(jnp.int32, (tile_count, tile_count), 1)
    earlier = (targets[:, None] == targets[None, :]) & (col_order < row_order)
    slot_rank = jnp.sum(earlier.astype(jnp.int32), axis=1)
    position = targets * capacity + slot_rank

    def to_slots(values):
        return jnp.zeros((slot_total,) + values.shape[1:], values.dtype).at[position].set(values)

    placing = jnp.stack([offsets[0, :, 0], offsets[0, :, 1], visits[0]], axis=1)
    placing_in = lax.all_to_all(to_slots(placing), "patch", split_axis=0, concat_axis=0, tiled=True)
    matched_here = match_psf(
        flat_tiles.reshape(tile_count, TILE, TILE), psf_coeff[0], row_taps, col_taps
    )
    matched, rows_in, cols_in = (
        lax.all_to_all(
            to_slots(matched_here.reshape(tile_count, TILE * TILE)),
            "patch",
            split_axis=0,
            concat_axis=0,
            tiled=True,
        ),
        lax.all_to_all(to_slots(warp_rows[0]), "patch", split_axis=0, concat_axis=0, tiled=True),
        lax.all_to_all(to_slots(warp_cols[0]), "patch", split_axis=0, concat_axis=0, tiled=True),
    )
    grouped = 32
    slot_items = (
        matched.reshape(-1, grouped, TILE, TILE),
        rows_in.reshape(-1, grouped, BW, TILE),
        cols_in.reshape(-1, grouped, BW, TILE),
        placing_in.reshape(-1, grouped, 3),
    )
    empty = jnp.zeros((PATCH, PATCH), jnp.float32)
    (numerator, coverage), _ = lax.scan(warp_block, (empty, empty), slot_items)
    coadd_image = numerator / jnp.maximum(coverage, 1.0)
    weighted = band_weight[0] * coadd_image
    detection = lax.psum(detect_sources(weighted, det_taps), "band")
    return (coadd_image[None], detection)


def solution(mesh):
    in_specs = (
        P("band", "patch", None),
        P("band", "patch", None),
        P(),
        P(),
        P("band", "patch", None),
        P("band", "patch", None),
        P("band", "patch"),
        P("band", "patch", None),
        P("band", "patch", None),
        P(),
        P("band"),
    )
    out_specs = (P("band", "patch", None), P("patch", None))
    return jax.shard_map(body, mesh=mesh, in_specs=in_specs, out_specs=out_specs, check_vma=False)
```

profile of v0, /device:TPU:1, one launch (start us, length us, event | category | flops | bytes accessed | tf_op | source)
XLA Modules:
  0.0 579.7 jit_solution(4976850623221434970)
XLA Ops:
  11.6 16.3 %all-to-all-start = ((s32[128,2,3]{2,1,0:T(2,128)}), s32[128,2,3]{2,1,0:T(2,128)S(1)}, u32[]{:S(2)}, u32[]{:S(2)}) async-start(s32[128,2,3]{2,1,0:T(2,128)} %bitcast.17), calls=%async_computation | async-start | bytes 262144 | tf_op jit(solution)/shard_map/all_to_all | solution.py:151
  30.5 8.7 %all-to-all-done = s32[128,2,3]{2,1,0:T(2,128)S(1)} async-done(((s32[128,2,3]{2,1,0:T(2,128)}), s32[128,2,3]{2,1,0:T(2,128)S(1)}, u32[]{:S(2)}, u32[]{:S(2)}) %all-to-all-start) | async-done | bytes 3104 | tf_op jit(solution)/shard_map/all_to_all | solution.py:151
  39.2 6.2 %all-to-all-start.1 = ((bf16[128,2,512]{2,1,0:T(2,128)(2,1)}), bf16[128,2,512]{2,1,0:T(2,128)(2,1)S(1)}, u32[]{:S(2)}, u32[]{:S(2)}) async-start(bf16[128,2,512]{2,1,0:T(2,128)(2,1)} %all_to_all.26), calls=%async_computation.1 | async-start | bytes 524288 | tf_op jit(solution)/shard_map/all_to_all | solution.py:163
  45.4 57.4 %gather_fusion = bf16[16384,5]{1,0:T(8,128)(2,1)} fusion(bf16[5,41]{0,1:T(8,128)(2,1)S(1)} %copy.54, s32[16384]{0:T(1024)S(1)} %bitcast_clamp_fusion), kind=kCustom, calls=%fused_computation.clone | custom fusion | bytes 393216 | tf_op jit(solution)/shard_map/jit(_take)/gather | solution.py:36
  102.8 3.9 copy.55
  106.8 57.4 %gather_fusion.1 = bf16[16384,5]{1,0:T(8,128)(2,1)} fusion(bf16[5,41]{0,1:T(8,128)(2,1)S(1)} %copy.57, s32[16384]{0:T(1024)S(1)} %bitcast_clamp_fusion), kind=kCustom, calls=%fused_computation.1.clone | custom fusion | bytes 393216 | tf_op jit(solution)/shard_map/jit(_take)/gather | solution.py:36
  164.2 3.8 copy.58
  171.9 13.4 %all-to-all-start.3 = ((bf16[128,2,512]{2,1,0:T(2,128)(2,1)}), bf16[128,2,512]{2,1,0:T(2,128)(2,1)S(1)}, u32[]{:S(2)}, u32[]{:S(2)}) async-start(bf16[128,2,512]{2,1,0:T(2,128)(2,1)} %all_to_all.30), calls=%async_computation.3 | async-start | bytes 524288 | tf_op jit(solution)/shard_map/all_to_all | solution.py:164
  185.3 11.9 %while.23 = (s32[]{:T(128)}, bf16[2,32,128,128]{3,2,1,0:T(8,128)(2,1)}, bf16[2,32,128,128]{3,2,1,0:T(8,128)(2,1)}, bf16[5,128,128]{2,1,0:T(8,128)(2,1)S(1)}, bf1...) while((s32[]{:T(128)}, bf16[2,32,128,128]{3,2,1,0:T(8,128)(2,1)}, ...), condition=%wide.region_2.4_spmd, body=%wide.region_1.3_spmd.sunk | while | flops 1347944576 | bytes 6621841 | solution.py:58
  185.3 4.2 fusion.248
  191.3 4.2 fusion.248
  197.1 10.1 %scatter_custom_fusion.2 = bf16[256,16384]{1,0:T(8,128)(2,1)} fusion(s32[64]{0:T(128)S(1)} %fusion.202, bf16[]{:T(256)} %constant.45.clone.1, bf16[8,8,128,128]{3,2,1,0:T(8,128)(2,1)} %bitcast.221), kind=kCustom, calls=%fused_computation.70 | custom fusion | bytes 10485762 | tf_op jit(solution)/shard_map/scatter | solution.py:148
  207.3 14.1 %all_to_all.28 = bf16[128,2,16384]{2,1,0:T(2,128)(2,1)} reshape(bf16[256,16384]{1,0:T(8,128)(2,1)} %scatter_custom_fusion.2) | data formatting | bytes 16777216 | tf_op jit(solution)/shard_map/all_to_all | solution.py:156
  221.4 13.8 %all-to-all-start.2 = ((bf16[128,2,16384]{2,1,0:T(2,128)(2,1)}), bf16[128,2,16384]{2,1,0:T(2,128)(2,1)}, u32[]{:S(2)}, u32[]{:S(2)}) async-start(bf16[128,2,16384]{2,1,0:T(2,128)(2,1)} %all_to_all.28), calls=%async_computation.2 | async-start | bytes 16777216 | tf_op jit(solution)/shard_map/all_to_all | solution.py:156
  236.3 178.9 %all-to-all-done.2 = bf16[128,2,16384]{2,1,0:T(2,128)(2,1)} async-done(((bf16[128,2,16384]{2,1,0:T(2,128)(2,1)}), bf16[128,2,16384]{2,1,0:T(2,128)(2,1)}, u32[]{:S(2)}, u32[]{:S(2)}) %all-to-all-start.2) | async-done | bytes 8388640 | tf_op jit(solution)/shard_map/all_to_all | solution.py:156
  415.2 14.5 %reshape.179 = bf16[8,32,128,128]{3,2,1,0:T(8,128)(2,1)} reshape(bf16[128,2,16384]{2,1,0:T(2,128)(2,1)} %all-to-all-done.2) | data formatting | bytes 16777216 | tf_op jit(solution)/shard_map/reshape | solution.py:168
  429.8 81.4 %while.24 = (s32[]{:T(128)}, f32[256,256]{1,0:T(8,128)S(1)}, f32[256,256]{1,0:T(8,128)S(1)}, s32[8,32,3]{1,2,0:T(4,128)S(1)}, bf16[8,32,4,128]{3,2,1,0:T(4,128)(...) while((s32[]{:T(128)}, f32[256,256]{1,0:T(8,128)S(1)}, ...), condition=%wide.region_10.12_spmd.clone, body=%wide.region_7.11_spmd.clone.sunk | while | flops 896811072 | bytes 2952048 | solution.py:174
  431.8 2.2 convert_reduce_fusion.5
  434.6 5.3 fusion.255
  442.0 2.2 convert_reduce_fusion.5
  444.8 5.3 fusion.255
  455.0 5.3 fusion.255
  465.1 5.3 fusion.255
  475.3 5.3 fusion.255
  485.5 5.3 fusion.255
  495.7 5.3 fusion.255
  505.9 5.3 fusion.255
  511.9 3.9 collective-permute-start
  517.8 2.3 collective-permute-done.1
  520.2 6.3 %fusion.61 = f32[256,256]{1,0:T(8,128)S(1)} fusion(f32[4,256]{1,0:T(4,128)S(1)} %collective-permute-done.1, f32[256,256]{1,0:T(8,128)S(1)} %get-tuple-element.167, f32[4,256]{1,0:T(4,128)S(1)} %collective-permute-done, f32[]{:T(128)} %bitcast.33, f32[]{:T(128)} %bitcast.34, f32[]{:T(128)} %bitcast.35, f32[]{:T(128)} %bitcast.36, f32[]{:T(128)} %bitcast.37, ...), kind=kOutput, calls=%fused_computation.82 | convolution fusion | flops 210051072 | bytes 532516 | tf_op jit(solution)/shard_map/dot_general | solution.py:118
  526.5 6.8 %fusion.104 = f32[256,256]{1,0:T(8,128)} fusion(f32[256,256]{1,0:T(8,128)S(1)} %fusion.61, f32[]{:T(128)} %bitcast.33, f32[]{:T(128)} %bitcast.34, f32[]{:T(128)} %bitcast.35, f32[]{:T(128)} %bitcast.36, f32[]{:T(128)} %bitcast.37, f32[]{:T(128)} %bitcast.39, f32[]{:T(128)} %bitcast.38, f32[]{:T(128)} %bitcast.30, f32[]{:T(128)} %bitcast.32), kind=kOutput, calls=%fused_computation.115 | convolution fusion | flops 203685888 | bytes 524324 | tf_op jit(solution)/shard_map/dot_general | solution.py:119
  533.4 37.9 %all-reduce.2.cloned.1.call-done = f32[256,256]{1,0:T(8,128)} async-done(((f32[256,256]{1,0:T(8,128)}), f32[256,256]{1,0:T(8,128)}) %all-reduce.2.cloned.1.call-update) | async-done | bytes 262160 | tf_op jit(solution)/shard_map/psum | solution.py:177
  (129 shorter events, 53.1 us)
Async XLA Ops:
  7.2 21.6 %copy-start = (bf16[1,64,512]{2,1,0:T(8,128)(2,1)S(1)}, bf16[1,64,512]{2,1,0:T(8,128)(2,1)}, u32[]{:S(2)}) copy-start(bf16[1,64,512]{2,1,0:T(8,128)(2,1)} %param.24) | copy-start | bytes 196612
  7.2 99.5 %copy-start.4 = (bf16[5,41]{1,0:T(8,128)(2,1)S(1)}, bf16[5,41]{1,0:T(8,128)(2,1)}, u32[]{:S(2)}) copy-start(bf16[5,41]{1,0:T(8,128)(2,1)} %param.19) | copy-start | bytes 1234
  11.6 27.6 %all-to-all-start = ((s32[128,2,3]{2,1,0:T(2,128)}), s32[128,2,3]{2,1,0:T(2,128)S(1)}, u32[]{:S(2)}, u32[]{:S(2)}) async-start(s32[128,2,3]{2,1,0:T(2,128)} %bitcast.17), calls=%async_computation | async-start | bytes 262144 | tf_op jit(solution)/shard_map/all_to_all | solution.py:151
  39.2 132.7 %all-to-all-start.1 = ((bf16[128,2,512]{2,1,0:T(2,128)(2,1)}), bf16[128,2,512]{2,1,0:T(2,128)(2,1)S(1)}, u32[]{:S(2)}, u32[]{:S(2)}) async-start(bf16[128,2,512]{2,1,0:T(2,128)(2,1)} %all_to_all.26), calls=%async_computation.1 | async-start | bytes 524288 | tf_op jit(solution)/shard_map/all_to_all | solution.py:163
  102.8 65.2 %copy-start.1 = (bf16[1,64,16384]{2,1,0:T(8,128)(2,1)S(1)}, bf16[1,64,16384]{2,1,0:T(8,128)(2,1)}, u32[]{:S(2)}) copy-start(bf16[1,64,16384]{2,1,0:T(8,128)(2,1)} %param.17) | copy-start | bytes 6291460
  164.2 5.7 copy-start.5
  164.2 5.8 %copy-start.2 = (bf16[1,64,512]{2,1,0:T(8,128)(2,1)S(1)}, bf16[1,64,512]{2,1,0:T(8,128)(2,1)}, u32[]{:S(2)}) copy-start(bf16[1,64,512]{2,1,0:T(8,128)(2,1)} %param.25) | copy-start | bytes 196612
  171.9 49.5 %all-to-all-start.3 = ((bf16[128,2,512]{2,1,0:T(2,128)(2,1)}), bf16[128,2,512]{2,1,0:T(2,128)(2,1)S(1)}, u32[]{:S(2)}, u32[]{:S(2)}) async-start(bf16[128,2,512]{2,1,0:T(2,128)(2,1)} %all_to_all.30), calls=%async_computation.3 | async-start | bytes 524288 | tf_op jit(solution)/shard_map/all_to_all | solution.py:164
  221.4 193.8 %all-to-all-start.2 = ((bf16[128,2,16384]{2,1,0:T(2,128)(2,1)}), bf16[128,2,16384]{2,1,0:T(2,128)(2,1)}, u32[]{:S(2)}, u32[]{:S(2)}) async-start(bf16[128,2,16384]{2,1,0:T(2,128)(2,1)} %all_to_all.28), calls=%async_computation.2 | async-start | bytes 16777216 | tf_op jit(solution)/shard_map/all_to_all | solution.py:156
  235.2 336.1 %all-reduce.2.cloned.1.call-start = ((), (), s32[]{:S(2)}) async-start(), calls=%async_computation.4 | async-start | bytes 524288 | tf_op jit(solution)/shard_map/psum | solution.py:177
  429.8 87.4 %copy-start.3 = (f32[9]{0:T(128)S(1)}, f32[9]{0:T(128)}, u32[]{:S(2)}) copy-start(f32[9]{0:T(128)} %param.26) | copy-start | bytes 112
  511.9 5.9 %collective-permute-start = (f32[4,256]{1,0:T(4,128)S(1)}, f32[4,256]{1,0:T(4,128)S(1)}, u32[]{:S(2)}, u32[]{:S(2)}) collective-permute-start(f32[4,256]{1,0:T(4,128)S(1)} %get-tuple-element.169), channel_id=1, source_target_pairs={{0,1},{1,2},{2,3},{3,4},{4,5},{5,6},{6,7},{7,8},{8,9},{9,10},{10,1... | collective-permute-start | bytes 12296 | tf_op jit(solution)/shard_map/ppermute | solution.py:21
  515.8 4.4 collective-permute-start.1
Sparse Core Ops, SparseCore 0:
  533.5 37.6 all-reduce.1
where the time goes:
time: 582 us; the launch traced here: 580 us
  waiting for transfers between devices  228 us (39%)
  local copies, waits for them, and re-layouts  177 us (30%)
  matrix products  68.1 us (12%)
  starting transfers between devices  54.9 us (9%)
  other arithmetic  36.7 us (6%)
  between operations  14.9 us (3%)
    all_to_all x1, waiting for transfers between devices, body(): lax.all_to_all(to_slots(matched_here.reshape(tile_count, TILE * TILE)), '...  179 us
    gather x4, local copies, waits for them, and re-layouts, band_matrix(): picked = jnp.take(taps, jnp.clip(offset, 0, taps.shape[-1] - 1), axis=-1)  122 us
    dot_general x8, matrix products, warp_block(): jnp.dot(rowmat.reshape(patch_edge, slot_count * tile_edge), shifted.resha...  42.5 us
    psum x1, waiting for transfers between devices, body(): detection = lax.psum(detect_sources(weighted, det_taps), 'band')  37.9 us
    reduce_sum x8, other arithmetic, warp_block(): rowsum = jnp.sum(rowmat.astype(jnp.float32), axis=2)  17.9 us
    all_to_all x1, starting transfers between devices, body(): lax.all_to_all(to_slots(placing), 'patch', split_axis=0, concat_axis=0, t...  16.3 us
    reduce_sum x8, other arithmetic, warp_block(): colsum = jnp.sum(colmat.astype(jnp.float32), axis=2)  15.5 us
    reshape x1, local copies, waits for them, and re-layouts, body(): matched.reshape(-1, grouped, TILE, TILE)  14.5 us
  transfers between devices with their start and end apart: 7, of which 4 were waited for; matrix products, arithmetic and copies ran while one was open for 26% of the time, Pallas kernels for 0%

commit v1 on v0

v1 whole, which is shorter than its diff:
```python
import functools

import jax
import jax.numpy as jnp
from jax import lax
from jax.experimental import pallas as pl
from jax.experimental.pallas import tpu as pltpu
from jax.sharding import PartitionSpec as P

TILE = 128
BW = 4
PATCH = 256
NTILE = 64
NBASIS = 5
TAPS = 41
NCLASS = 8
CAP = 32
SLOT = 144
WIN = 144
FAC = 16
PROWS = PATCH + FAC
ZROWS = PATCH + 4 * FAC
NZ = 8
MESH = pl.DeviceIdType.MESH
MIB = 1 << 20

bf16, f32, i32 = jnp.bfloat16, jnp.float32, jnp.int32
CONTRACT_LAST = (((1,), (1,)), ((), ()))
CONTRACT_FIRST = (((0,), (0,)), ((), ()))


def coords():
    me = lax.axis_index("patch")
    return me, me // 16, (me // 4) % 4, me % 4


def match_kernel(info, coef, tiles, rtaps, ctaps, wrows, wcols, slots, meta, buf, wr32, wc32, gcat, hstack, counts, sems):
    for k in range(NBASIS):
        for taps, is_row in ((rtaps, True), (ctaps, False)):
            line = taps[k : k + 1, :].astype(f32)
            line = jnp.concatenate([line, jnp.zeros((1, 2 * TILE - TAPS), f32)], axis=1)
            full = jnp.broadcast_to(line, (TILE, 2 * TILE))
            full = pltpu.roll(full, 2 * TILE - (TAPS - 1) // 2, 1)
            full = pltpu.roll(full, 0, 1, stride=1, stride_axis=0)
            band = full[:, :TILE].astype(bf16)
            if is_row:
                gcat[:, k * TILE : (k + 1) * TILE] = band
            else:
                hstack[k * TILE : (k + 1) * TILE, :] = band
    wr32[...] = wrows[...].astype(f32)
    wc32[...] = wcols[...].astype(f32)
    for c in range(NCLASS):
        counts[c] = 0

    def placed(line, offset):
        wide = jnp.concatenate([line, jnp.zeros((BW, TILE), f32)], axis=1)
        wide = jnp.concatenate([wide, jnp.zeros((8 - BW, 2 * TILE), f32)], axis=0)
        summed = jnp.sum(pltpu.roll(wide, 0, 1, stride=1, stride_axis=0), axis=0, keepdims=True)
        return pltpu.roll(summed, offset, 1)

    def tapped(line):
        return jnp.concatenate([line[:, b * TILE : (b + 1) * TILE] for b in range(BW)], axis=0)

    def copy_of(t, position):
        return pltpu.make_async_copy(buf.at[t], slots.at[position], sems.at[t])

    def pair(i, carry):
        images = tiles[pl.ds(2 * i, 2)].reshape(2 * TILE, TILE)
        part = lax.dot_general(images, hstack[...], CONTRACT_LAST, preferred_element_type=f32)
        columns = []
        for u in range(2):
            rows = part[u * TILE : (u + 1) * TILE]
            columns.append(
                jnp.concatenate(
                    [
                        (rows[:, k * TILE : (k + 1) * TILE] * coef[(2 * i + u) * NBASIS + k]).astype(bf16)
                        for k in range(NBASIS)
                    ],
                    axis=0,
                )
            )
        scaled = jnp.concatenate(columns, axis=1)
        matched = jnp.dot(gcat[...], scaled, preferred_element_type=f32).astype(bf16)
        for u in range(2):
            t = 2 * i + u
            target, off_r, off_c, visit = info[t], info[NTILE + t], info[2 * NTILE + t], info[3 * NTILE + t]
            pz, px, py = target // 16, (target // 4) % 4, target % 4
            even = (pz % 2) == 0
            group = jnp.where(even, px, 4 + py)
            inner = jnp.where(even, py, px) * 4 + pz // 2 + jnp.where(even, 0, 16)
            rank = counts[group]
            counts[group] = rank + 1
            meta[group, 0, rank * 4] = inner
            meta[group, 0, rank * 4 + 1] = off_r
            meta[group, 0, rank * 4 + 2] = off_c
            row_line = tapped((wr32[pl.ds(t, 1), :] * visit.astype(f32)).astype(bf16).astype(f32))
            col_line = tapped(wc32[pl.ds(t, 1), :])
            row_sum = placed(row_line, off_r)
            col_sum = placed(col_line, off_c)
            tail = jnp.concatenate(
                [
                    row_line,
                    col_line,
                    row_sum[:, :TILE],
                    row_sum[:, TILE:],
                    col_sum[:, :TILE],
                    col_sum[:, TILE:],
                    jnp.zeros((4, TILE), f32),
                ],
                axis=0,
            )
            buf[t, :TILE, :] = matched[:, u * TILE : (u + 1) * TILE]
            buf[t, TILE:, :] = tail.astype(bf16)
            copy_of(t, group * 32 + rank).start()
        return carry

    lax.fori_loop(0, NTILE // 2, pair, 0)
    for c in range(NCLASS):
        meta[c, 0, 3] = counts[c]

    def finish(t, carry):
        copy_of(t, 0).wait()
        return carry

    lax.fori_loop(0, NTILE, finish, 0)


def match_tiles(info, coef, tiles, rtaps, ctaps, wrows, wcols):
    smem = pl.BlockSpec(memory_space=pltpu.SMEM)
    vmem = pl.BlockSpec(memory_space=pltpu.VMEM)
    return pl.pallas_call(
        match_kernel,
        out_shape=(
            jax.ShapeDtypeStruct((NCLASS * 32, SLOT, TILE), bf16),
            jax.ShapeDtypeStruct((NCLASS, 1, 128), i32),
        ),
        in_specs=[smem, smem] + [vmem] * 5,
        out_specs=(pl.BlockSpec(memory_space=pl.ANY), smem),
        scratch_shapes=[
            pltpu.VMEM((NTILE, SLOT, TILE), bf16),
            pltpu.VMEM((NTILE, BW * TILE), f32),
            pltpu.VMEM((NTILE, BW * TILE), f32),
            pltpu.VMEM((TILE, NBASIS * TILE), bf16),
            pltpu.VMEM((NBASIS * TILE, TILE), bf16),
            pltpu.SMEM((NCLASS,), i32),
            pltpu.SemaphoreType.DMA((NTILE,)),
        ],
        compiler_params=pltpu.CompilerParams(vmem_limit_bytes=40 * MIB),
        name="match",
    )(info, coef, tiles, rtaps, ctaps, wrows, wcols)


def ring_neighbours():
    me, z, x, y = coords()
    return (
        (x, z * 16 + ((x + 1) % 4) * 4 + y, z * 16 + ((x + 3) % 4) * 4 + y),
        (y, z * 16 + x * 4 + (y + 1) % 4, z * 16 + x * 4 + (y + 3) % 4),
    )


def greet(partners):
    barrier = pltpu.get_barrier_semaphore()
    for partner in partners:
        pl.semaphore_signal(barrier, inc=1, device_id=partner, device_id_type=MESH)
    pl.semaphore_wait(barrier, len(partners))


def remote(src, dst, send, recv, patch):
    return pltpu.make_async_remote_copy(
        src_ref=src, dst_ref=dst, send_sem=send, recv_sem=recv, device_id={"patch": patch}, device_id_type=MESH
    )


def ring_exchange(send_block, recv_block, relays, half, size, sends, recvs, first):
    rings = ring_neighbours()
    out, onward = [], []
    n = first
    for a, (here, plus, minus) in enumerate(rings):
        across = (here + 2) % 4
        out.append(remote(send_block(a, across, 0, half), relays.at[2 * a], sends.at[n], recvs.at[n], plus))
        out.append(
            remote(send_block(a, across, half, size - half), relays.at[2 * a + 1], sends.at[n + 1], recvs.at[n + 1], minus)
        )
        n += 2
    for a, (here, plus, minus) in enumerate(rings):
        out.append(
            remote(send_block(a, (here + 1) % 4, 0, size), recv_block(a, here, 0, size), sends.at[n], recvs.at[n], plus)
        )
        out.append(
            remote(send_block(a, (here + 3) % 4, 0, size), recv_block(a, here, 0, size), sends.at[n + 1], recvs.at[n + 1], minus)
        )
        n += 2
    for a, (here, plus, minus) in enumerate(rings):
        onward.append(
            remote(relays.at[2 * a], recv_block(a, (here + 3) % 4, 0, half), sends.at[n], recvs.at[n], plus)
        )
        onward.append(
            remote(relays.at[2 * a + 1], recv_block(a, (here + 1) % 4, half, size - half), sends.at[n + 1], recvs.at[n + 1], minus)
        )
        n += 2
    return out, onward


def route_kernel(cap, slots, meta, recv, rmeta, relays, meta_relays, sends, recvs, local):
    rings = ring_neighbours()
    greet([{"patch": p} for ring in rings for p in ring[1:]])
    own = []
    for a, (here, _, _) in enumerate(rings):
        own.append(pltpu.make_async_copy(slots.at[4 * a + here, pl.ds(0, cap)], recv.at[4 * a + here], local.at[2 * a]))
        own.append(pltpu.make_async_copy(meta.at[4 * a + here], rmeta.at[4 * a + here], local.at[2 * a + 1]))
    mout, monward = [], []
    n = 12
    for a, (here, plus, minus) in enumerate(rings):
        mout.append(remote(meta.at[4 * a + (here + 2) % 4], meta_relays.at[a], sends.at[n], recvs.at[n], plus))
        mout.append(remote(meta.at[4 * a + (here + 1) % 4], rmeta.at[4 * a + here], sends.at[n + 1], recvs.at[n + 1], plus))
        mout.append(remote(meta.at[4 * a + (here + 3) % 4], rmeta.at[4 * a + here], sends.at[n + 2], recvs.at[n + 2], minus))
        monward.append(remote(meta_relays.at[a], rmeta.at[4 * a + (here + 3) % 4], sends.at[n + 3], recvs.at[n + 3], plus))
        n += 4
    out, onward = ring_exchange(
        lambda a, i, start, size: slots.at[4 * a + i, pl.ds(start, size)],
        lambda a, i, start, size: recv.at[4 * a + i, pl.ds(start, size)],
        relays,
        cap // 2,
        cap,
        sends,
        recvs,
        0,
    )
    for copy in mout + out + own:
        copy.start()
    for a in range(2):
        mout[3 * a].wait_recv()
        monward[a].start()
    for i in range(4):
        out[i].wait_recv()
        onward[i].start()
    for i in range(4):
        out[i].wait_send()
    for copy in out[4:]:
        copy.wait()
    for a in range(2):
        mout[3 * a].wait_send()
        mout[3 * a + 1].wait()
        mout[3 * a + 2].wait()
    for copy in monward + onward + own:
        copy.wait()


def route_tiles(slots, meta, cap, collective_id):
    hbm = pl.BlockSpec(memory_space=pl.ANY)
    return pl.pallas_call(
        functools.partial(route_kernel, cap),
        out_shape=(
            jax.ShapeDtypeStruct((NCLASS, cap, SLOT, TILE), bf16),
            jax.ShapeDtypeStruct((NCLASS, 1, 128), i32),
        ),
        in_specs=[hbm, hbm],
        out_specs=(hbm, hbm),
        scratch_shapes=[
            pltpu.VMEM((4, cap // 2, SLOT, TILE), bf16),
            pltpu.VMEM((2, 1, 128), i32),
            pltpu.SemaphoreType.DMA((20,)),
            pltpu.SemaphoreType.DMA((20,)),
            pltpu.SemaphoreType.DMA((4,)),
        ],
        compiler_params=pltpu.CompilerParams(
            collective_id=collective_id, has_side_effects=True, vmem_limit_bytes=40 * MIB
        ),
        name="route",
    )(slots.reshape(NCLASS, 32, SLOT, TILE), meta)


UNROLL = 4


def warp_kernel(cap, meta, recv, out, acc, fac, names, fill):
    acc[...] = jnp.zeros_like(acc)
    fac[...] = jnp.zeros_like(fac)
    for p in range(32):
        fill[p] = 0
    total = jnp.int32(0)
    for c in range(NCLASS):
        here = meta[c, 0, 3]

        def note(s, carry, c=c, total=total):
            names[total + s] = c * cap + s
            return carry

        lax.fori_loop(0, here, note, 0)
        total = total + here
    gap = lax.broadcasted_iota(i32, (PATCH, TILE), 0) - lax.broadcasted_iota(i32, (PATCH, TILE), 1)

    def banded(lines, first, gaps, offset):
        gaps = gaps - offset
        mat = jnp.zeros(gaps.shape, f32)
        for b in range(BW):
            mat = jnp.where(gaps == b, lines[first + b : first + b + 1, :], mat)
        return mat.astype(bf16)

    place = lax.broadcasted_iota(i32, (8, TILE), 0)

    def step(i, carry):
        todo = []
        for u in range(UNROLL):
            n = i * UNROLL + u
            slot = names[jnp.minimum(n, total - 1)]
            group, rank = slot // cap, slot % cap
            inner = meta[group, 0, rank * 4]
            off_r = meta[group, 0, rank * 4 + 1]
            off_c = meta[group, 0, rank * 4 + 2]
            tail = recv[group, rank, TILE:, :].astype(f32)
            live = jnp.where(n < total, 1.0, 0.0).astype(f32)
            colmat = banded(tail, BW, gap, off_c)
            shifted = lax.dot_general(
                recv[group, rank, :TILE, :], colmat, CONTRACT_LAST, preferred_element_type=f32
            ).astype(bf16)
            aligned = pl.multiple_of(jnp.minimum((off_r // 8) * 8, PATCH - WIN), 8)
            rowmat = banded(tail * live, 0, gap[:WIN], off_r - aligned)
            todo.append((n, inner, aligned, tail, jnp.dot(rowmat, shifted, preferred_element_type=f32)))
        for n, inner, aligned, tail, term in todo:
            acc[inner, pl.ds(aligned, WIN), :] += term

            at = fill[inner]
            fill[inner] = at + jnp.where(n < total, 1, 0)
            chosen = jnp.where(n < total, at, FAC)
            for k in range(4):
                rows, lanes = pl.ds(8 * (k // 2), 8), pl.ds(TILE * (k % 2), TILE)
                old = fac[inner, rows, lanes]
                fac[inner, rows, lanes] = jnp.where(place == chosen, tail[8 + k : 9 + k], old)

        return carry

    lax.fori_loop(0, (total + UNROLL - 1) // UNROLL, step, 0)

    def store(p, carry):
        out[p, :PATCH, :] = acc[p].astype(bf16)
        out[p, PATCH:, :] = fac[p].astype(bf16)
        return carry

    lax.fori_loop(0, 32, store, 0)


def warp_tiles(meta, recv, cap):
    return pl.pallas_call(
        functools.partial(warp_kernel, cap),
        out_shape=jax.ShapeDtypeStruct((32, PROWS, PATCH), bf16),
        in_specs=[pl.BlockSpec(memory_space=pltpu.SMEM), pl.BlockSpec(memory_space=pltpu.VMEM)],
        out_specs=pl.BlockSpec(memory_space=pltpu.VMEM),
        scratch_shapes=[
            pltpu.VMEM((32, PATCH, PATCH), f32),
            pltpu.VMEM((32, FAC, PATCH), f32),
            pltpu.SMEM((NCLASS * 32,), i32),
            pltpu.SMEM((32,), i32),
        ],
        compiler_params=pltpu.CompilerParams(vmem_limit_bytes=50 * MIB),
        name="warp",
    )(meta, recv)


def merge_kernel(
    part, taps, weight, coadd, detection, recv, relays, zpart, zrecv, mine, other, halo, rowk, colk, sends, recvs, local
):
    me, z, x, y = coords()
    band = lax.axis_index("band")
    rings = ring_neighbours()
    above, below = (me + 127) % 128, (me + 1) % 128
    partners = [{"patch": p} for ring in rings for p in ring[1:]]
    partners += [{"patch": ((z + d) % NZ) * 16 + x * 4 + y} for d in range(1, NZ)]
    partners += [{"patch": me, "band": 1 - band}]
    partners += [{"patch": p, "band": b} for p in (above, below) for b in (band, 1 - band)]
    greet(partners)
    out, onward = ring_exchange(
        lambda a, i, start, size: part.at[1 - a, i, pl.ds(start, size)],
        lambda a, i, start, size: recv.at[1 - a, i, pl.ds(start, size)],
        relays,
        2,
        4,
        sends,
        recvs,
        0,
    )
    own = [
        pltpu.make_async_copy(part.at[0, y], recv.at[0, y], local.at[0]),
        pltpu.make_async_copy(part.at[1, x], recv.at[1, x], local.at[1]),
    ]
    for copy in out + own:
        copy.start()
    wide = PATCH + 16
    row_gap = lax.broadcasted_iota(i32, (PATCH, wide), 1) - lax.broadcasted_iota(i32, (PATCH, wide), 0) - 4
    col_gap = lax.broadcasted_iota(i32, (PATCH, PATCH), 0) - lax.broadcasted_iota(i32, (PATCH, PATCH), 1) + 4
    row_kernel = jnp.zeros((PATCH, wide), f32)
    col_kernel = jnp.zeros((PATCH, PATCH), f32)
    for r in range(9):
        row_kernel = jnp.where(row_gap == r, taps[r], row_kernel)
        col_kernel = jnp.where(col_gap == r, taps[r], col_kernel)
    rowk[...] = row_kernel
    colk[...] = col_kernel
    for i in range(4):
        out[i].wait_recv()
        onward[i].start()
    for i in range(4):
        out[i].wait_send()
    for copy in out[4:] + onward + own:
        copy.wait()

    for a in range(2):
        def fold(zz, carry, a=a):
            total = jnp.zeros((PATCH, PATCH), f32)
            for s in range(4):
                total = total + recv[a, s, zz, :PATCH, :].astype(f32)
                zpart[2 * zz + a, PATCH + s * FAC : PATCH + (s + 1) * FAC, :] = recv[a, s, zz, PATCH:, :]
            zpart[2 * zz + a, :PATCH, :] = total.astype(bf16)
            return carry

        lax.fori_loop(0, 4, fold, 0)

    zcopies = []
    for d in range(1, NZ):
        to = (z + d) % NZ
        copy = remote(zpart.at[to], zrecv.at[z], sends.at[11 + d], recvs.at[11 + d], to * 16 + x * 4 + y)
        copy.start()
        zcopies.append(copy)
    own = pltpu.make_async_copy(zpart.at[z], zrecv.at[z], local.at[0])
    own.start()
    own.wait()
    for copy in zcopies:
        copy.wait()
    total = jnp.zeros((PATCH, PATCH), f32)
    row_sums, col_sums = [], []
    for s in range(NZ):
        total = total + zrecv[s, :PATCH, :].astype(f32)
        sums = zrecv[s, PATCH:, :].astype(f32)
        for q in range(4):
            row_sums.append(sums[q * FAC : q * FAC + 8])
            col_sums.append(sums[q * FAC + 8 : (q + 1) * FAC])
    cover = lax.dot_general(
        jnp.concatenate(row_sums, axis=0).astype(bf16),
        jnp.concatenate(col_sums, axis=0).astype(bf16),
        CONTRACT_FIRST,
        preferred_element_type=f32,
    )
    image = total / jnp.maximum(cover, 1.0)
    coadd[...] = image
    mine[...] = image * weight[0]

    def to_core(src, dst, n, patch, core):
        return pltpu.make_async_remote_copy(
            src_ref=src,
            dst_ref=dst,
            send_sem=sends.at[n],
            recv_sem=recvs.at[n],
            device_id={"patch": patch, "band": core},
            device_id_type=MESH,
        )

    last = [
        to_core(mine.at[pl.ds(PATCH - 8, 8)], halo.at[0, 0], 19, below, band),
        to_core(mine.at[pl.ds(PATCH - 8, 8)], halo.at[0, 1], 20, below, 1 - band),
        to_core(mine.at[pl.ds(0, 8)], halo.at[1, 0], 21, above, band),
        to_core(mine.at[pl.ds(0, 8)], halo.at[1, 1], 22, above, 1 - band),
        to_core(mine, other, 23, me, 1 - band),
    ]
    for copy in last:
        copy.start()
    for copy in last:
        copy.wait()
    top = jnp.where(me == 0, 0.0, halo[0, 0] + halo[0, 1])
    bottom = jnp.where(me == 127, 0.0, halo[1, 0] + halo[1, 1])
    padded = jnp.concatenate([top, mine[...] + other[...], bottom], axis=0)
    row_pass = jnp.dot(rowk[...], padded, precision=lax.Precision.HIGHEST, preferred_element_type=f32)
    detection[...] = jnp.dot(row_pass, colk[...], precision=lax.Precision.HIGHEST, preferred_element_type=f32)


def merge(part, det_taps, band_weight):
    smem = pl.BlockSpec(memory_space=pltpu.SMEM)
    vmem = pl.BlockSpec(memory_space=pltpu.VMEM)
    image = jax.ShapeDtypeStruct((PATCH, PATCH), f32)
    return pl.pallas_call(
        merge_kernel,
        out_shape=(image, image),
        in_specs=[pl.BlockSpec(memory_space=pl.ANY), smem, smem],
        out_specs=(vmem, vmem),
        scratch_shapes=[
            pltpu.VMEM((2, 4, 4, PROWS, PATCH), bf16),
            pltpu.VMEM((4, 2, PROWS, PATCH), bf16),
            pltpu.VMEM((NZ, ZROWS, PATCH), bf16),
            pltpu.VMEM((NZ, ZROWS, PATCH), bf16),
            pltpu.VMEM((PATCH, PATCH), f32),
            pltpu.VMEM((PATCH, PATCH), f32),
            pltpu.VMEM((2, 2, 8, PATCH), f32),
            pltpu.VMEM((PATCH, PATCH + 16), f32),
            pltpu.VMEM((PATCH, PATCH), f32),
            pltpu.SemaphoreType.DMA((24,)),
            pltpu.SemaphoreType.DMA((24,)),
            pltpu.SemaphoreType.DMA((2,)),
        ],
        compiler_params=pltpu.CompilerParams(collective_id=2, has_side_effects=True, vmem_limit_bytes=50 * MIB),
        name="merge",
    )(part.reshape(2, 4, 4, PROWS, PATCH), det_taps, band_weight)


def body(
    tiles, psf_coeff, row_taps, col_taps, target_patch, offsets, visits, warp_rows, warp_cols, det_taps, band_weight
):
    info = jnp.concatenate([target_patch[0, :, 0], offsets[0, :, 0], offsets[0, :, 1], visits[0]])
    coef = psf_coeff[0].astype(f32).reshape(-1)
    slots, meta = match_tiles(
        info, coef, tiles[0].reshape(NTILE, TILE, TILE), row_taps, col_taps, warp_rows[0], warp_cols[0]
    )
    recv, rmeta = route_tiles(slots, meta, CAP, 0)
    part = warp_tiles(rmeta, recv, CAP)
    coadd, detection = merge(part, det_taps, band_weight)
    return coadd[None], detection


def solution(mesh):
    in_specs = (
        P("band", "patch", None),
        P("band", "patch", None),
        P(),
        P(),
        P("band", "patch", None),
        P("band", "patch", None),
        P("band", "patch"),
        P("band", "patch", None),
        P("band", "patch", None),
        P(),
        P("band"),
    )
    out_specs = (P("band", "patch", None), P("patch", None))
    return jax.shard_map(body, mesh=mesh, in_specs=in_specs, out_specs=out_specs, check_vma=False)
```

time: 582 us -> 192 us (0.33)
  waiting for transfers between devices: 228 us -> 0 us
  Pallas kernels: 0 us -> 173 us
  local copies, waits for them, and re-layouts: 177 us -> 15.5 us
  matrix products: 68.1 us -> 0 us
  starting transfers between devices: 54.9 us -> 0 us
  other arithmetic: 36.7 us -> 0.75 us
  between operations: 14.9 us -> 1.35 us
    all_to_all x4 -> x0, waiting for transfers between devices: 188 us -> none  [the longest x1 179 us: body(): lax.all_to_all(to_slots(matched_here.reshape(tile_count, TILE * TILE)), '...]
    pallas_call x0 -> x4, Pallas kernels: none -> 173 us  [the longest x1 71.5 us: merge(): pl.pallas_call(merge_kernel, out_shape=(image, image), in_specs=[pl.Block...]
    gather x5 -> x0, local copies, waits for them, and re-layouts: 123 us -> none  [the longest x4 122 us: band_matrix(): picked = jnp.take(taps, jnp.clip(offset, 0, taps.shape[-1] - 1), axis=-1)]
    dot_general x20 -> x0, matrix products: 68.1 us -> none  [the longest x8 42.5 us: warp_block(): jnp.dot(rowmat.reshape(patch_edge, slot_count * tile_edge), shifted.resha...]
    all_to_all x4 -> x0, starting transfers between devices: 49.6 us -> none  [the longest x1 16.3 us: body(): lax.all_to_all(to_slots(placing), 'patch', split_axis=0, concat_axis=0, t...]
    psum x1 -> x0, waiting for transfers between devices: 37.9 us -> none  [body(): detection = lax.psum(detect_sources(weighted, det_taps), 'band')]
    reduce_sum x17 -> x0, other arithmetic: 34.3 us -> none  [the longest x8 17.9 us: warp_block(): rowsum = jnp.sum(rowmat.astype(jnp.float32), axis=2)]
    all_to_all x3 -> x0, local copies, waits for them, and re-layouts: 15.7 us -> none  [the longest x1 14.1 us: body(): lax.all_to_all(to_slots(matched_here.reshape(tile_count, TILE * TILE)), '...]
  transfers between devices with their start and end apart: 7 -> 0, of which waited for: 4 -> 0; matrix products, arithmetic and copies ran while one was open for 26% -> 0% of each run, Pallas kernels for 0% -> 0%
where the time goes in v1:
time: 192 us; the launch traced here: 191 us
  Pallas kernels  173 us (90%)
  local copies, waits for them, and re-layouts  15.5 us (8%)
    pallas_call x1, Pallas kernels, merge(): pl.pallas_call(merge_kernel, out_shape=(image, image), in_specs=[pl.Block...  71.5 us
    pallas_call x1, Pallas kernels, route_tiles(): pl.pallas_call(functools.partial(route_kernel, cap), out_shape=(jax.Shape...  57.4 us
    pallas_call x1, Pallas kernels, match_tiles(): pl.pallas_call(match_kernel, out_shape=(jax.ShapeDtypeStruct((NCLASS * 32...  25.1 us
    pallas_call x1, Pallas kernels, warp_tiles(): pl.pallas_call(functools.partial(warp_kernel, cap), out_shape=jax.ShapeDt...  19.2 us
    unnamed x17, local copies, waits for them, and re-layouts  13.9 us

profile of v1, /device:TPU:1, one launch (start us, length us, event | category | flops | bytes accessed | tf_op | source)
XLA Modules:
  0.0 190.8 jit_solution(2806372685575364140)
XLA Ops:
  0.6 0.8 slice_bitcast_fusion.1
  1.4 0.7 pad_add_fusion.info
  2.1 2.2 %copy.14 = bf16[8,8,128,128]{3,2,1,0:T(8,128)(2,1)S(1)} copy(bf16[8,8,128,128]{3,1,2,0:T(8,128)(2,1)} %bitcast.20) | data formatting | bytes 4194304
  4.3 0.8 copy.13
  5.1 0.1 reshape.16.coef
  5.2 0.0 copy-start.2
  5.2 0.8 copy-done.2
  6.1 0.0 copy-start.3
  6.1 0.8 copy-done.3
  6.9 0.0 copy-start.4
  6.9 0.7 copy-done.4
  7.6 0.0 copy-start.5
  7.6 0.7 copy-done.5
  8.3 25.1 %match.1 = (bf16[256,144,128]{2,1,0:T(8,128)(2,1)S(1)}, s32[8,1,128]{2,1,0:T(1,128)S(1)}) custom-call(s32[256]{0:T(256)S(1)} %pad_add_fusion.info, f32[320]{0:T(512)S(1)} %reshape.16.coef, bf16[64,128,128]{2,1,0:T(8,128)(2,1)S(1)} %bitcast.15, bf16[5,41]{1,0:T(8,128)(2,1)S(1)} %copy-done.4, bf16[5,41]{1,0:T(8,128)(2,1)S(1)} %copy-done.5, ...), custom_call_target="tpu_custom_call" | custom-call | tf_op jit(solution)/shard_map/match/pallas_call | solution.py:131
  33.4 0.0 copy-start
  33.4 3.6 %copy-done = bf16[256,144,128]{2,1,0:T(8,128)(2,1)} copy-done((bf16[256,144,128]{2,1,0:T(8,128)(2,1)}, bf16[256,144,128]{2,1,0:T(8,128)(2,1)S(1)}, u32[]{:S(2)}) %copy-start) | copy-done | bytes 9437208
  37.0 57.4 %route.1 = (bf16[8,32,144,128]{3,2,1,0:T(8,128)(2,1)S(1)}, s32[8,1,128]{2,1,0:T(1,128)S(1)}) custom-call(bf16[8,32,144,128]{3,2,1,0:T(8,128)(2,1)} %bitcast.14, s32[8,1,128]{2,1,0:T(1,128)S(1)} %get-tuple-element.9.meta), custom_call_target="tpu_custom_call" | custom-call | tf_op jit(solution)/shard_map/route/pallas_call | solution.py:251
  94.4 0.0 copy-start.1
  94.4 3.6 %copy-done.1 = bf16[8,32,144,128]{3,2,1,0:T(8,128)(2,1)} copy-done((bf16[8,32,144,128]{3,2,1,0:T(8,128)(2,1)}, bf16[8,32,144,128]{3,2,1,0:T(8,128)(2,1)S(1)}, u32[]{:S(2)}) %copy-start.1) | copy-done | bytes 9437208
  98.0 0.0 copy-start.6
  98.0 19.2 %warp.1 = bf16[32,272,256]{2,1,0:T(8,128)(2,1)} custom-call(s32[8,1,128]{2,1,0:T(1,128)S(1)} %get-tuple-element.10.meta, bf16[8,32,144,128]{3,2,1,0:T(8,128)(2,1)} %copy-done.1), custom_call_target="tpu_custom_call" | custom-call | tf_op jit(solution)/shard_map/warp/pallas_call | solution.py:344
  117.9 0.0 copy-done.6
  117.9 71.5 %merge.1 = (f32[256,256]{1,0:T(8,128)S(1)}, f32[256,256]{1,0:T(8,128)S(1)}) custom-call(bf16[2,4,4,272,256]{4,3,2,1,0:T(8,128)(2,1)} %bitcast.19, f32[9]{0:T(128)S(1)} %copy-done.6, f32[1]{0:T(128)S(6)} %copy.17.weight), custom_call_target="tpu_custom_call" | custom-call | tf_op jit(solution)/shard_map/merge/pallas_call | solution.py:478
  189.4 0.7 copy.18
  190.1 0.7 copy.19
Async XLA Ops:
  5.2 0.8 copy-start.2
  6.1 0.8 copy-start.3
  6.9 0.7 copy-start.4
  7.6 0.7 copy-start.5
  33.4 3.6 %copy-start = (bf16[256,144,128]{2,1,0:T(8,128)(2,1)}, bf16[256,144,128]{2,1,0:T(8,128)(2,1)S(1)}, u32[]{:S(2)}) copy-start(bf16[256,144,128]{2,1,0:T(8,128)(2,1)S(1)} %get-tuple-element.8) | copy-start | bytes 28311556
  94.4 3.6 %copy-start.1 = (bf16[8,32,144,128]{3,2,1,0:T(8,128)(2,1)}, bf16[8,32,144,128]{3,2,1,0:T(8,128)(2,1)S(1)}, u32[]{:S(2)}) copy-start(bf16[8,32,144,128]{3,2,1,0:T(8,128)(2,1)S(1)} %get-tuple-element.11.recv) | copy-start | bytes 28311556
  98.0 19.8 %copy-start.6 = (f32[9]{0:T(128)S(1)}, f32[9]{0:T(128)}, u32[]{:S(2)}) copy-start(f32[9]{0:T(128)} %taps.1) | copy-start | bytes 112

commit v2 on v1

v2 whole, which is shorter than its diff:
```python
import functools

import jax
import jax.numpy as jnp
from jax import lax
from jax.experimental import pallas as pl
from jax.experimental.pallas import tpu as pltpu
from jax.sharding import PartitionSpec as P

TILE = 128
BW = 4
PATCH = 256
NTILE = 64
NBASIS = 5
TAPS = 41
NCLASS = 8
CAP = 16
SLOT = 144
WIN = 144
FAC = 16
PROWS = PATCH + FAC
ZROWS = PATCH + 4 * FAC
NZ = 8
NCHUNK = 4
CHUNK = PATCH // NCHUNK
MESH = pl.DeviceIdType.MESH
MIB = 1 << 20
STEPS = 8

bf16, f32, i32 = jnp.bfloat16, jnp.float32, jnp.int32
CONTRACT_LAST = (((1,), (1,)), ((), ()))
CONTRACT_FIRST = (((0,), (0,)), ((), ()))


def coords():
    me = lax.axis_index("patch")
    return me, me // 16, (me // 4) % 4, me % 4


def match_kernel(
    info, coef, tiles, rtaps, ctaps, wrows, wcols, slots, meta,
    images, rows16, cols16, wr32, wc32, gcat, hstack, counts, places, loads,
):
    chunk = NTILE // STEPS

    def load_of(i):
        part = pl.ds(i * chunk, chunk)
        return pltpu.make_async_copy(tiles.at[part], images.at[part], loads.at[i])

    weights = [
        pltpu.make_async_copy(wrows, rows16, loads.at[STEPS]),
        pltpu.make_async_copy(wcols, cols16, loads.at[STEPS + 1]),
    ]
    for copy in weights + [load_of(i) for i in range(STEPS)]:
        copy.start()
    for k in range(NBASIS):
        for taps, is_row in ((rtaps, True), (ctaps, False)):
            line = taps[k : k + 1, :].astype(f32)
            line = jnp.concatenate([line, jnp.zeros((1, 2 * TILE - TAPS), f32)], axis=1)
            full = jnp.broadcast_to(line, (TILE, 2 * TILE))
            full = pltpu.roll(full, 2 * TILE - (TAPS - 1) // 2, 1)
            full = pltpu.roll(full, 0, 1, stride=1, stride_axis=0)
            band = full[:, :TILE].astype(bf16)
            if is_row:
                gcat[:, k * TILE : (k + 1) * TILE] = band
            else:
                hstack[k * TILE : (k + 1) * TILE, :] = band
    for c in range(NCLASS):
        counts[c] = 0

    def assign(t, carry):
        target = info[t]
        pz, px, py = target // 16, (target // 4) % 4, target % 4
        even = (pz % 2) == 0
        group = jnp.where(even, px, 4 + py)
        rank = counts[group]
        counts[group] = rank + 1
        places[t] = group * 32 + rank
        meta[group, 0, rank * 4] = jnp.where(even, py, px) * 4 + pz // 2 + jnp.where(even, 0, 16)
        meta[group, 0, rank * 4 + 1] = info[NTILE + t]
        meta[group, 0, rank * 4 + 2] = info[2 * NTILE + t]
        return carry

    lax.fori_loop(0, NTILE, assign, 0)
    for c in range(NCLASS):
        meta[c, 0, 3] = counts[c]
    for copy in weights:
        copy.wait()
    wr32[...] = rows16[...].astype(f32)
    wc32[...] = cols16[...].astype(f32)

    def placed(line, offset):
        wide = jnp.concatenate([line, jnp.zeros((BW, TILE), f32)], axis=1)
        wide = jnp.concatenate([wide, jnp.zeros((8 - BW, 2 * TILE), f32)], axis=0)
        summed = jnp.sum(pltpu.roll(wide, 0, 1, stride=1, stride_axis=0), axis=0, keepdims=True)
        return pltpu.roll(summed, offset, 1)

    def tapped(line):
        return jnp.concatenate([line[:, b * TILE : (b + 1) * TILE] for b in range(BW)], axis=0)

    def pack(i, carry):
        for u in range(4):
            t = 4 * i + u
            off_r, off_c, visit = info[NTILE + t], info[2 * NTILE + t], info[3 * NTILE + t]
            row_line = tapped((wr32[pl.ds(t, 1), :] * visit.astype(f32)).astype(bf16).astype(f32))
            col_line = tapped(wc32[pl.ds(t, 1), :])
            row_sum = placed(row_line, off_r)
            col_sum = placed(col_line, off_c)
            tail = [row_line, col_line]
            tail += [row_sum[:, :TILE], row_sum[:, TILE:], col_sum[:, :TILE], col_sum[:, TILE:]]
            tail += [jnp.zeros((4, TILE), f32)]
            slots[places[t], TILE:, :] = jnp.concatenate(tail, axis=0).astype(bf16)
        return carry

    lax.fori_loop(0, NTILE // 4, pack, 0)

    def step(i, carry):
        load_of(i).wait()
        for v in range(chunk // 2):
            first = i * chunk + 2 * v
            pair = images[pl.ds(first, 2)].reshape(2 * TILE, TILE)
            part = lax.dot_general(pair, hstack[...], CONTRACT_LAST, preferred_element_type=f32)
            columns = []
            for u in range(2):
                rows = part[u * TILE : (u + 1) * TILE]
                blocks = [
                    (rows[:, k * TILE : (k + 1) * TILE] * coef[(first + u) * NBASIS + k]).astype(bf16)
                    for k in range(NBASIS)
                ]
                columns.append(jnp.concatenate(blocks, axis=0))
            scaled = jnp.concatenate(columns, axis=1)
            matched = jnp.dot(gcat[...], scaled, preferred_element_type=f32).astype(bf16)
            for u in range(2):
                slots[places[first + u], :TILE, :] = matched[:, u * TILE : (u + 1) * TILE]
        return carry

    lax.fori_loop(0, STEPS, step, 0)


def match_tiles(info, coef, tiles, rtaps, ctaps, wrows, wcols):
    smem = pl.BlockSpec(memory_space=pltpu.SMEM)
    vmem = pl.BlockSpec(memory_space=pltpu.VMEM)
    hbm = pl.BlockSpec(memory_space=pl.ANY)
    return pl.pallas_call(
        match_kernel,
        out_shape=(
            jax.ShapeDtypeStruct((NCLASS * 32, SLOT, TILE), bf16),
            jax.ShapeDtypeStruct((NCLASS, 1, 128), i32),
        ),
        in_specs=[smem, smem, hbm, vmem, vmem, hbm, hbm],
        out_specs=(vmem, smem),
        scratch_shapes=[
            pltpu.VMEM((NTILE, TILE, TILE), bf16),
            pltpu.VMEM((NTILE, BW * TILE), bf16),
            pltpu.VMEM((NTILE, BW * TILE), bf16),
            pltpu.VMEM((NTILE, BW * TILE), f32),
            pltpu.VMEM((NTILE, BW * TILE), f32),
            pltpu.VMEM((TILE, NBASIS * TILE), bf16),
            pltpu.VMEM((NBASIS * TILE, TILE), bf16),
            pltpu.SMEM((NCLASS,), i32),
            pltpu.SMEM((NTILE,), i32),
            pltpu.SemaphoreType.DMA((STEPS + 2,)),
        ],
        compiler_params=pltpu.CompilerParams(vmem_limit_bytes=14 * MIB),
        name="match",
    )(info, coef, tiles, rtaps, ctaps, wrows, wcols)


def greet(partners):
    barrier = pltpu.get_barrier_semaphore()
    for partner in partners:
        pl.semaphore_signal(barrier, inc=1, device_id=partner, device_id_type=MESH)
    pl.semaphore_wait(barrier, len(partners))


def remote(src, dst, send, recv, patch):
    return pltpu.make_async_remote_copy(
        src_ref=src, dst_ref=dst, send_sem=send, recv_sem=recv, device_id={"patch": patch}, device_id_type=MESH
    )


def ring_copies(send_block, recv_block, sends, recvs, first):
    me, z, x, y = coords()
    copies = []
    for d in (2, 1, 3):
        for axis, here in ((0, x), (1, y)):
            there = (here + d) % 4
            owner = z * 16 + there * 4 + y if axis == 0 else z * 16 + x * 4 + there
            n = first + len(copies)
            copies.append(remote(send_block(axis, there), recv_block(axis, here), sends.at[n], recvs.at[n], owner))
    return copies


def ring_partners():
    me, z, x, y = coords()
    partners = [{"patch": z * 16 + ((x + d) % 4) * 4 + y} for d in (1, 2, 3)]
    return partners + [{"patch": z * 16 + x * 4 + (y + d) % 4} for d in (1, 2, 3)]


def column_partners():
    me, z, x, y = coords()
    return [{"patch": ((z + d) % NZ) * 16 + x * 4 + y} for d in range(1, NZ)]


def to_device(src, dst, send, recv, device):
    return pltpu.make_async_remote_copy(
        src_ref=src, dst_ref=dst, send_sem=send, recv_sem=recv, device_id=device, device_id_type=MESH
    )


def route_kernel(cap, slots, meta, recv, rmeta, most, loads, box_x, box_y, box_z, box_b, sends, recvs, local):
    me, z, x, y = coords()
    band = lax.axis_index("band")
    rings, column = ring_partners(), column_partners()
    sibling = {"patch": me, "band": 1 - band}
    greet(rings + column + [sibling])
    small = ring_copies(lambda a, i: meta.at[4 * a + i], lambda a, i: rmeta.at[4 * a + i], sends, recvs, 6)
    for n, own in enumerate((x, 4 + y)):
        small.append(pltpu.make_async_copy(meta.at[own], rmeta.at[own], local.at[n]))
    large = ring_copies(
        lambda a, i: slots.at[4 * a + i, pl.ds(0, cap)], lambda a, i: recv.at[4 * a + i], sends, recvs, 0
    )
    fetch = pltpu.make_async_copy(meta, loads, local.at[2])
    fetch.start()
    for copy in small:
        copy.start()
    fetch.wait()
    top = jnp.max(loads[...], axis=0)
    n = 12
    for box, here, others in (
        (box_x, x, rings[:3]),
        (box_y, y, rings[3:]),
        (box_z, z, column),
        (box_b, band, [sibling]),
    ):
        box[here] = top
        shared = []
        for other in others:
            shared.append(to_device(box.at[here], box.at[here], sends.at[n], recvs.at[n], other))
            n += 1
        for copy in shared:
            copy.start()
        if box is box_y:
            for copy in large:
                copy.start()
        for copy in shared:
            copy.wait()
        top = jnp.max(box[...], axis=0)
    most[...] = top
    for copy in small + large:
        copy.wait()


def route_tiles(slots, meta, cap, collective_id):
    hbm = pl.BlockSpec(memory_space=pl.ANY)
    return pl.pallas_call(
        functools.partial(route_kernel, cap),
        out_shape=(
            jax.ShapeDtypeStruct((NCLASS, cap, SLOT, TILE), bf16),
            jax.ShapeDtypeStruct((NCLASS, 1, 128), i32),
            jax.ShapeDtypeStruct((1, 128), i32),
        ),
        in_specs=[hbm, hbm],
        out_specs=(hbm, hbm, pl.BlockSpec(memory_space=pltpu.VMEM)),
        scratch_shapes=[
            pltpu.VMEM((NCLASS, 1, 128), i32),
            pltpu.VMEM((4, 1, 128), i32),
            pltpu.VMEM((4, 1, 128), i32),
            pltpu.VMEM((NZ, 1, 128), i32),
            pltpu.VMEM((2, 1, 128), i32),
            pltpu.SemaphoreType.DMA((26,)),
            pltpu.SemaphoreType.DMA((26,)),
            pltpu.SemaphoreType.DMA((3,)),
        ],
        compiler_params=pltpu.CompilerParams(
            collective_id=collective_id, has_side_effects=True, vmem_limit_bytes=4 * MIB
        ),
        name="route",
    )(slots.reshape(NCLASS, 32, SLOT, TILE), meta)


UNROLL = 4


def warp_kernel(cap, meta, recv, slots, out, acc, fac, names, fill):
    _, _, x, y = coords()
    for p in range(32):
        fill[p] = 0

    total = jnp.int32(0)
    for c in range(NCLASS):
        here = meta[c, 0, 3]

        def note(s, carry, c=c, total=total):
            names[total + s] = c * 32 + s
            return carry

        lax.fori_loop(0, here, note, 0)
        total = total + here
    acc[...] = jnp.zeros_like(acc)
    fac[...] = jnp.zeros_like(fac)
    gap = lax.broadcasted_iota(i32, (PATCH, TILE), 0) - lax.broadcasted_iota(i32, (PATCH, TILE), 1)

    def banded(lines, first, gaps, offset):
        gaps = gaps - offset
        mat = jnp.zeros(gaps.shape, f32)
        for b in range(BW):
            mat = jnp.where(gaps == b, lines[first + b : first + b + 1, :], mat)
        return mat.astype(bf16)

    place = lax.broadcasted_iota(i32, (8, TILE), 0)

    def step(i, carry):
        todo = []
        for u in range(UNROLL):
            n = i * UNROLL + u
            at = jnp.minimum(n, total - 1)
            slot = names[at]
            group, rank = slot // 32, slot % 32
            inner = meta[group, 0, rank * 4]
            off_r = meta[group, 0, rank * 4 + 1]
            off_c = meta[group, 0, rank * 4 + 2]
            kept = (group == x) | (group == 4 + y)
            image = jnp.where(kept, slots[slot], recv[group, rank])
            tail = image[TILE:, :].astype(f32)
            live = jnp.where(n < total, 1.0, 0.0).astype(f32)
            colmat = banded(tail, BW, gap, off_c)
            shifted = lax.dot_general(
                image[:TILE, :], colmat, CONTRACT_LAST, preferred_element_type=f32
            ).astype(bf16)
            aligned = pl.multiple_of(jnp.minimum((off_r // 8) * 8, PATCH - WIN), 8)
            rowmat = banded(tail * live, 0, gap[:WIN], off_r - aligned)
            todo.append((n, inner, aligned, tail, jnp.dot(rowmat, shifted, preferred_element_type=f32)))
        for n, inner, aligned, tail, term in todo:
            acc[inner, pl.ds(aligned, WIN), :] += term

            at = fill[inner]
            fill[inner] = at + jnp.where(n < total, 1, 0)
            chosen = jnp.where(n < total, at, FAC)
            for k in range(4):
                rows, lanes = pl.ds(8 * (k // 2), 8), pl.ds(TILE * (k % 2), TILE)
                old = fac[inner, rows, lanes]
                fac[inner, rows, lanes] = jnp.where(place == chosen, tail[8 + k : 9 + k], old)

        return carry

    lax.fori_loop(0, (total + UNROLL - 1) // UNROLL, step, 0)

    def store(p, carry):
        out[p, FAC:, :] = acc[p].astype(bf16)
        out[p, :FAC, :] = fac[p].astype(bf16)
        return carry

    lax.fori_loop(0, 32, store, 0)


def warp_tiles(meta, recv, slots, cap):
    vmem = pl.BlockSpec(memory_space=pltpu.VMEM)
    return pl.pallas_call(
        functools.partial(warp_kernel, cap),
        out_shape=jax.ShapeDtypeStruct((32, PROWS, PATCH), bf16),
        in_specs=[pl.BlockSpec(memory_space=pltpu.SMEM), vmem, vmem],
        out_specs=vmem,
        scratch_shapes=[
            pltpu.VMEM((32, PATCH, PATCH), f32),
            pltpu.VMEM((32, FAC, PATCH), f32),
            pltpu.SMEM((NCLASS * 32,), i32),
            pltpu.SMEM((32,), i32),
        ],
        compiler_params=pltpu.CompilerParams(vmem_limit_bytes=18 * MIB),
        name="warp",
    )(meta, recv, slots)


def merge_kernel(
    part, taps, weight, coadd, detection, recv, zpart, zrecv, mine, other, halo, rowk, colk, sends, recvs
):
    me, z, x, y = coords()
    band = lax.axis_index("band")
    above, below = (me + 127) % 128, (me + 1) % 128
    column = column_partners()
    sibling = {"patch": me, "band": 1 - band}
    near = [{"patch": p, "band": b} for p in (above, below) for b in (band, 1 - band)]
    greet(ring_partners() + column + [sibling] + near)

    def rows_of(c, lead):
        start = 0 if c == 0 else lead + c * CHUNK
        return pl.ds(start, lead + CHUNK if c == 0 else CHUNK)

    def ring_part(c):
        rows = rows_of(c, FAC)
        copies = ring_copies(
            lambda a, i: part.at[1 - a, i, pl.ds(0, 4), rows],
            lambda a, i: recv.at[1 - a, i, pl.ds(0, 4), rows],
            sends,
            recvs,
            6 * c,
        )
        for copy in copies:
            copy.start()
        return copies

    pending = [ring_part(0), ring_part(1)]
    wide = PATCH + 16
    row_gap = lax.broadcasted_iota(i32, (PATCH, wide), 1) - lax.broadcasted_iota(i32, (PATCH, wide), 0) - 4
    col_gap = lax.broadcasted_iota(i32, (PATCH, PATCH), 0) - lax.broadcasted_iota(i32, (PATCH, PATCH), 1) + 4
    row_kernel = jnp.zeros((PATCH, wide), f32)
    col_kernel = jnp.zeros((PATCH, PATCH), f32)
    for r in range(9):
        row_kernel = jnp.where(row_gap == r, taps[r], row_kernel)
        col_kernel = jnp.where(col_gap == r, taps[r], col_kernel)
    rowk[...] = row_kernel
    colk[...] = col_kernel

    zcopies = []
    for c in range(NCHUNK):
        for copy in pending[c]:
            copy.wait()
        if c + 2 < NCHUNK:
            pending.append(ring_part(c + 2))
        for a in range(2):

            own = x if a else y

            def fold(zz, carry, a=a, c=c, own=own):
                if c == 0:
                    zpart[2 * zz + a, :FAC, :] = part[a, own, zz, :FAC, :]
                    for d in range(1, 4):
                        zpart[2 * zz + a, d * FAC : (d + 1) * FAC, :] = recv[a, (own + d) % 4, zz, :FAC, :]
                chunk = pl.ds(FAC + c * CHUNK, CHUNK)
                total = part[a, own, zz, chunk, :].astype(f32)
                for d in range(1, 4):
                    total = total + recv[a, (own + d) % 4, zz, chunk, :].astype(f32)
                at = 4 * FAC + c * CHUNK
                zpart[2 * zz + a, at : at + CHUNK, :] = total.astype(bf16)
                return carry

            lax.fori_loop(0, 4, fold, 0)
        rows = rows_of(c, 4 * FAC)
        copies = []
        for d in (4, 3, 5, 2, 6, 1, 7):
            to = (z + d) % NZ
            n = 6 * NCHUNK + 7 * c + d - 1
            copies.append(
                remote(zpart.at[to, rows], zrecv.at[z, rows], sends.at[n], recvs.at[n], to * 16 + x * 4 + y)
            )
        for copy in copies:
            copy.start()
        zcopies.append(copies)

    cover = None
    last = []
    base = 13 * NCHUNK
    for c in range(NCHUNK):
        for copy in zcopies[c]:
            copy.wait()
        if c == 0:
            row_sums, col_sums = [], []
            for d in range(NZ):
                sums = (zrecv[(z + d) % NZ, : 4 * FAC, :] if d else zpart[z, : 4 * FAC, :]).astype(f32)
                for q in range(4):
                    row_sums.append(sums[q * FAC : q * FAC + 8])
                    col_sums.append(sums[q * FAC + 8 : (q + 1) * FAC])
            cover = lax.dot_general(
                jnp.concatenate(row_sums, axis=0).astype(bf16),
                jnp.concatenate(col_sums, axis=0).astype(bf16),
                CONTRACT_FIRST,
                preferred_element_type=f32,
            )
            mine[...] = jnp.maximum(cover, 1.0)
        chunk = pl.ds(4 * FAC + c * CHUNK, CHUNK)
        total = zpart[z, chunk, :].astype(f32)
        for d in range(1, NZ):
            total = total + zrecv[(z + d) % NZ, chunk, :].astype(f32)
        rows = slice(c * CHUNK, (c + 1) * CHUNK)
        image = total / mine[rows, :]
        coadd[rows, :] = image
        mine[rows, :] = image * weight[0]
        ship = pl.ds(c * CHUNK, CHUNK)
        copies = [to_device(mine.at[ship], other.at[ship], sends.at[base + c], recvs.at[base + c], sibling)]
        if c == 0:
            for n in (0, 1):
                k = base + NCHUNK + n
                copies.append(to_device(mine.at[pl.ds(0, 8)], halo.at[1, n], sends.at[k], recvs.at[k], near[n]))
        if c == NCHUNK - 1:
            for n in (0, 1):
                k = base + NCHUNK + 2 + n
                copies.append(
                    to_device(mine.at[pl.ds(PATCH - 8, 8)], halo.at[0, n], sends.at[k], recvs.at[k], near[2 + n])
                )
        for copy in copies:
            copy.start()
        last += copies
    for copy in last:
        copy.wait()
    top = jnp.where(me == 0, 0.0, halo[0, 0] + halo[0, 1])
    bottom = jnp.where(me == 127, 0.0, halo[1, 0] + halo[1, 1])
    padded = jnp.concatenate([top, mine[...] + other[...], bottom], axis=0)
    row_pass = jnp.dot(rowk[...], padded, precision=lax.Precision.HIGHEST, preferred_element_type=f32)
    detection[...] = jnp.dot(row_pass, colk[...], precision=lax.Precision.HIGHEST, preferred_element_type=f32)


def merge(part, det_taps, band_weight):
    smem = pl.BlockSpec(memory_space=pltpu.SMEM)
    vmem = pl.BlockSpec(memory_space=pltpu.VMEM)
    image = jax.ShapeDtypeStruct((PATCH, PATCH), f32)
    count = 14 * NCHUNK + 4
    return pl.pallas_call(
        merge_kernel,
        out_shape=(image, image),
        in_specs=[vmem, smem, smem],
        out_specs=(vmem, vmem),
        scratch_shapes=[
            pltpu.VMEM((2, 4, 4, PROWS, PATCH), bf16),
            pltpu.VMEM((NZ, ZROWS, PATCH), bf16),
            pltpu.VMEM((NZ, ZROWS, PATCH), bf16),
            pltpu.VMEM((PATCH, PATCH), f32),
            pltpu.VMEM((PATCH, PATCH), f32),
            pltpu.VMEM((2, 2, 8, PATCH), f32),
            pltpu.VMEM((PATCH, PATCH + 16), f32),
            pltpu.VMEM((PATCH, PATCH), f32),
            pltpu.SemaphoreType.DMA((count,)),
            pltpu.SemaphoreType.DMA((count,)),
        ],
        compiler_params=pltpu.CompilerParams(collective_id=2, has_side_effects=True, vmem_limit_bytes=14 * MIB),
        name="merge",
    )(part.reshape(2, 4, 4, PROWS, PATCH), det_taps, band_weight)


def body(
    tiles, psf_coeff, row_taps, col_taps, target_patch, offsets, visits, warp_rows, warp_cols, det_taps, band_weight
):
    info = jnp.concatenate([target_patch[0, :, 0], offsets[0, :, 0], offsets[0, :, 1], visits[0]])
    coef = psf_coeff[0].astype(f32).reshape(-1)
    slots, meta = match_tiles(
        info, coef, tiles[0].reshape(NTILE, TILE, TILE), row_taps, col_taps, warp_rows[0], warp_cols[0]
    )
    recv, rmeta, most = route_tiles(slots, meta, CAP, 0)

    def few():
        return warp_tiles(rmeta, recv, slots, CAP)

    def many():
        whole, wmeta, _ = route_tiles(slots, meta, 32, 1)
        return warp_tiles(wmeta, whole, slots, 32)

    part = lax.cond(most[0, 3] > CAP, many, few)
    coadd, detection = merge(part, det_taps, band_weight)
    return coadd[None], detection


def solution(mesh):
    in_specs = (
        P("band", "patch", None),
        P("band", "patch", None),
        P(),
        P(),
        P("band", "patch", None),
        P("band", "patch", None),
        P("band", "patch"),
        P("band", "patch", None),
        P("band", "patch", None),
        P(),
        P("band"),
    )
    out_specs = (P("band", "patch", None), P("patch", None))
    return jax.shard_map(body, mesh=mesh, in_specs=in_specs, out_specs=out_specs, check_vma=False)
```

time: 192 us -> 137 us (0.71)
  Pallas kernels: 173 us -> 125 us
  local copies, waits for them, and re-layouts: 15.5 us -> 8.87 us
    pallas_call x1, Pallas kernels: 71.5 us -> 54.1 us  [merge(): pl.pallas_call(merge_kernel, out_shape=(image, image), in_specs=[vmem, sm...]
    pallas_call x1, Pallas kernels: 57.4 us -> 41.3 us  [route_tiles(): pl.pallas_call(functools.partial(route_kernel, cap), out_shape=(jax.Shape...]
    pallas_call x1, Pallas kernels: 25.1 us -> 15.3 us  [match_tiles(): pl.pallas_call(match_kernel, out_shape=(jax.ShapeDtypeStruct((NCLASS * 32...]
    unnamed x17 -> x13, local copies, waits for them, and re-layouts: 13.9 us -> 6.61 us
    pallas_call x1, Pallas kernels: 19.2 us -> 14.8 us  [warp_tiles(): pl.pallas_call(functools.partial(warp_kernel, cap), out_shape=jax.ShapeDt...]
where the time goes in v2:
time: 137 us
  Pallas kernels  125 us (91%)
  local copies, waits for them, and re-layouts  8.87 us (6%)
  between operations  2 us (1%)
    pallas_call x1, Pallas kernels, merge(): pl.pallas_call(merge_kernel, out_shape=(image, image), in_specs=[vmem, sm...  54.1 us
    pallas_call x1, Pallas kernels, route_tiles(): pl.pallas_call(functools.partial(route_kernel, cap), out_shape=(jax.Shape...  41.3 us
    pallas_call x1, Pallas kernels, match_tiles(): pl.pallas_call(match_kernel, out_shape=(jax.ShapeDtypeStruct((NCLASS * 32...  15.3 us
    pallas_call x1, Pallas kernels, warp_tiles(): pl.pallas_call(functools.partial(warp_kernel, cap), out_shape=jax.ShapeDt...  14.8 us
    unnamed x13, local copies, waits for them, and re-layouts  6.61 us

profile of v2, /device:TPU:1, one launch (start us, length us, event | category | flops | bytes accessed | tf_op | source)
XLA Modules:
  0.0 137.1 jit_solution(18395368919139497998)
XLA Ops:
  0.6 0.8 slice_bitcast_fusion.1
  1.4 0.7 pad_add_fusion.info
  2.1 2.2 %copy.14 = bf16[8,8,128,128]{3,2,1,0:T(8,128)(2,1)S(1)} copy(bf16[8,8,128,128]{3,1,2,0:T(8,128)(2,1)} %bitcast.25) | data formatting | bytes 4194304
  4.3 0.8 copy.13
  5.1 0.1 reshape.24.coef
  5.2 0.0 copy-start
  5.2 0.8 copy-done
  6.1 0.0 copy-start.1
  6.1 0.8 copy-done.1
  6.9 0.0 copy-start.2
  6.9 0.7 copy-done.2
  7.6 0.0 copy-start.3
  7.6 0.7 copy-done.3
  8.3 15.3 %match.1 = (bf16[256,144,128]{2,1,0:T(8,128)(2,1)S(1)}, s32[8,1,128]{2,1,0:T(1,128)S(1)}) custom-call(s32[256]{0:T(256)S(1)} %pad_add_fusion.info, f32[320]{0:T(512)S(1)} %reshape.24.coef, bf16[64,128,128]{2,1,0:T(8,128)(2,1)S(1)} %bitcast.17, bf16[5,41]{1,0:T(8,128)(2,1)S(1)} %copy-done.2, bf16[5,41]{1,0:T(8,128)(2,1)S(1)} %copy-done.3, ...), custom_call_target="tpu_custom_call" | custom-call | tf_op jit(solution)/shard_map/match/pallas_call | solution.py:144
  23.6 41.3 %route.3 = (bf16[8,16,144,128]{3,2,1,0:T(8,128)(2,1)S(1)}, s32[8,1,128]{2,1,0:T(1,128)S(1)}, s32[1,128]{1,0:T(1,128)S(1)}) custom-call(bf16[8,32,144,128]{3,2,1,0:T(8,128)(2,1)S(1)} %bitcast.21, s32[8,1,128]{2,1,0:T(1,128)S(1)} %get-tuple-element.31.meta), custom_call_target="tpu_custom_call" | custom-call | tf_op jit(solution)/shard_map/route/pallas_call | solution.py:256
  64.9 0.6 slice.11
  66.1 0.0 copy-start.4
  66.1 14.8 %conditional.1 = (bf16[2,4,4,272,256]{4,3,2,1,0:T(8,128)(2,1)}) conditional(s32[]{:T(128)} %bitcast.10, (s32[8,1,128]{2,1,0:T(1,128)S(1)}, bf16[8,16,144,128]{3,2,1,0:T(8,128)(2,1)S(1)}, bf16[256,144,128]{2,1,0:T(8,128)(2,1)S(1)}) %tuple.15, (bf16[256,144,128]{2,1,0:T(8,128)(2,1)S(1)}, s32[8,1,128]{2,1,0:T(1,128)S(1)}) %match.1), branch_computations={%region_0.0_spmd, %region_1.0_spmd} | conditional | bytes 75497536 | solution.py:547
  66.1 14.8 %warp.2 = bf16[32,272,256]{2,1,0:T(8,128)(2,1)} custom-call(s32[8,1,128]{2,1,0:T(1,128)S(1)} %get-tuple-element.14.meta, bf16[8,16,144,128]{3,2,1,0:T(8,128)(2,1)S(1)} %get-tuple-element.15.recv, bf16[256,144,128]{2,1,0:T(8,128)(2,1)S(1)} %get-tuple-element.16.slots), custom_call_target="tpu_custom_call" | custom-call | tf_op jit(solution)/shard_map/cond/branch_0_fun/warp/pallas_call | solution.py:359
  81.5 0.0 copy-done.4
  81.5 54.1 %merge.1 = (f32[256,256]{1,0:T(8,128)S(1)}, f32[256,256]{1,0:T(8,128)S(1)}) custom-call(bf16[2,4,4,272,256]{4,3,2,1,0:T(8,128)(2,1)} %get-tuple-element.43.part, f32[9]{0:T(128)S(1)} %copy-done.4, f32[1]{0:T(128)S(6)} %copy.19.weight), custom_call_target="tpu_custom_call" | custom-call | tf_op jit(solution)/shard_map/merge/pallas_call | solution.py:508
  135.6 0.7 copy.20
  136.4 0.7 copy.21
Async XLA Ops:
  5.2 0.8 copy-start
  6.1 0.8 copy-start.1
  6.9 0.7 copy-start.2
  7.6 0.7 copy-start.3
  66.1 15.4 %copy-start.4 = (f32[9]{0:T(128)S(1)}, f32[9]{0:T(128)}, u32[]{:S(2)}) copy-start(f32[9]{0:T(128)} %taps.1) | copy-start | bytes 112

commit v3 on v2

--- a/solution.py
+++ b/solution.py
@@ -21,11 +21,11 @@
 PROWS = PATCH + FAC
 ZROWS = PATCH + 4 * FAC
 NZ = 8
-NCHUNK = 4
+NCHUNK = 8
 CHUNK = PATCH // NCHUNK
 MESH = pl.DeviceIdType.MESH
 MIB = 1 << 20
-STEPS = 8
+STEPS = 4
 
 bf16, f32, i32 = jnp.bfloat16, jnp.float32, jnp.int32
 CONTRACT_LAST = (((1,), (1,)), ((), ()))
@@ -38,8 +38,7 @@
 
 
 def match_kernel(
-    info, coef, tiles, rtaps, ctaps, wrows, wcols, slots, meta,
-    images, rows16, cols16, wr32, wc32, gcat, hstack, counts, places, loads,
+    info, packed, tiles, slots, meta, images, coef32, coef, gcat, hstack, wr32, wc32, counts, places, loads
 ):
     chunk = NTILE // STEPS
 
@@ -47,29 +46,29 @@
         part = pl.ds(i * chunk, chunk)
         return pltpu.make_async_copy(tiles.at[part], images.at[part], loads.at[i])
 
-    weights = [
-        pltpu.make_async_copy(wrows, rows16, loads.at[STEPS]),
-        pltpu.make_async_copy(wcols, cols16, loads.at[STEPS + 1]),
-    ]
-    for copy in weights + [load_of(i) for i in range(STEPS)]:
-        copy.start()
-    for k in range(NBASIS):
-        for taps, is_row in ((rtaps, True), (ctaps, False)):
-            line = taps[k : k + 1, :].astype(f32)
-            line = jnp.concatenate([line, jnp.zeros((1, 2 * TILE - TAPS), f32)], axis=1)
-            full = jnp.broadcast_to(line, (TILE, 2 * TILE))
-            full = pltpu.roll(full, 2 * TILE - (TAPS - 1) // 2, 1)
-            full = pltpu.roll(full, 0, 1, stride=1, stride_axis=0)
-            band = full[:, :TILE].astype(bf16)
-            if is_row:
+    for i in range(STEPS):
+        load_of(i).start()
+    coef32[...] = packed[2 * NTILE : 2 * NTILE + 8, :TILE].astype(f32)
+    scalars = pltpu.make_async_copy(coef32, coef, loads.at[STEPS])
+    scalars.start()
+    wr32[...] = packed[:NTILE, :].astype(f32)
+    wc32[...] = packed[NTILE : 2 * NTILE, :].astype(f32)
+    for n in range(2):
+        first = 2 * NTILE + 16 * (n + 1)
+        lines = packed[first : first + 16, : 2 * TILE].astype(f32)
+        lines = pltpu.roll(lines, 2 * TILE - (TAPS - 1) // 2, 1)
+        for k in range(NBASIS):
+            full = jnp.broadcast_to(lines[k : k + 1, :], (TILE, 2 * TILE))
+            band = pltpu.roll(full, 0, 1, stride=1, stride_axis=0)[:, :TILE].astype(bf16)
+            if n == 0:
                 gcat[:, k * TILE : (k + 1) * TILE] = band
             else:
                 hstack[k * TILE : (k + 1) * TILE, :] = band
     for c in range(NCLASS):
         counts[c] = 0
 
-    def assign(t, carry):
-        target = info[t]
+    for t in range(NTILE):
+        target = info[0, t]
         pz, px, py = target // 16, (target // 4) % 4, target % 4
         even = (pz % 2) == 0
         group = jnp.where(even, px, 4 + py)
@@ -77,18 +76,10 @@
         counts[group] = rank + 1
         places[t] = group * 32 + rank
         meta[group, 0, rank * 4] = jnp.where(even, py, px) * 4 + pz // 2 + jnp.where(even, 0, 16)
-        meta[group, 0, rank * 4 + 1] = info[NTILE + t]
-        meta[group, 0, rank * 4 + 2] = info[2 * NTILE + t]
-        return carry
-
-    lax.fori_loop(0, NTILE, assign, 0)
+        meta[group, 0, rank * 4 + 1] = info[1, t]
+        meta[group, 0, rank * 4 + 2] = info[2, t]
     for c in range(NCLASS):
         meta[c, 0, 3] = counts[c]
-    for copy in weights:
-        copy.wait()
-    wr32[...] = rows16[...].astype(f32)
-    wc32[...] = cols16[...].astype(f32)
-
     def placed(line, offset):
         wide = jnp.concatenate([line, jnp.zeros((BW, TILE), f32)], axis=1)
         wide = jnp.concatenate([wide, jnp.zeros((8 - BW, 2 * TILE), f32)], axis=0)
@@ -98,21 +89,16 @@
     def tapped(line):
         return jnp.concatenate([line[:, b * TILE : (b + 1) * TILE] for b in range(BW)], axis=0)
 
-    def pack(i, carry):
-        for u in range(4):
-            t = 4 * i + u
-            off_r, off_c, visit = info[NTILE + t], info[2 * NTILE + t], info[3 * NTILE + t]
-            row_line = tapped((wr32[pl.ds(t, 1), :] * visit.astype(f32)).astype(bf16).astype(f32))
-            col_line = tapped(wc32[pl.ds(t, 1), :])
-            row_sum = placed(row_line, off_r)
-            col_sum = placed(col_line, off_c)
-            tail = [row_line, col_line]
-            tail += [row_sum[:, :TILE], row_sum[:, TILE:], col_sum[:, :TILE], col_sum[:, TILE:]]
-            tail += [jnp.zeros((4, TILE), f32)]
-            slots[places[t], TILE:, :] = jnp.concatenate(tail, axis=0).astype(bf16)
-        return carry
-
-    lax.fori_loop(0, NTILE // 4, pack, 0)
+    def pack(t):
+        off_r, off_c, visit = info[1, t], info[2, t], info[3, t]
+        row_line = tapped((wr32[pl.ds(t, 1), :] * visit.astype(f32)).astype(bf16).astype(f32))
+        col_line = tapped(wc32[pl.ds(t, 1), :])
+        row_sum = placed(row_line, off_r)
+        col_sum = placed(col_line, off_c)
+        tail = [row_line, col_line]
+        tail += [row_sum[:, :TILE], row_sum[:, TILE:], col_sum[:, :TILE], col_sum[:, TILE:]]
+        tail += [jnp.zeros((4, TILE), f32)]
+        return jnp.concatenate(tail, axis=0).astype(bf16)
 
     def step(i, carry):
         load_of(i).wait()
@@ -124,46 +110,48 @@
             for u in range(2):
                 rows = part[u * TILE : (u + 1) * TILE]
                 blocks = [
-                    (rows[:, k * TILE : (k + 1) * TILE] * coef[(first + u) * NBASIS + k]).astype(bf16)
+                    (rows[:, k * TILE : (k + 1) * TILE] * coef[k, first + u]).astype(bf16)
                     for k in range(NBASIS)
                 ]
                 columns.append(jnp.concatenate(blocks, axis=0))
             scaled = jnp.concatenate(columns, axis=1)
             matched = jnp.dot(gcat[...], scaled, preferred_element_type=f32).astype(bf16)
             for u in range(2):
-                slots[places[first + u], :TILE, :] = matched[:, u * TILE : (u + 1) * TILE]
+                at = places[first + u]
+                slots[at, :TILE, :] = matched[:, u * TILE : (u + 1) * TILE]
+                slots[at, TILE:, :] = pack(first + u)
         return carry
 
+    scalars.wait()
     lax.fori_loop(0, STEPS, step, 0)
 
 
-def match_tiles(info, coef, tiles, rtaps, ctaps, wrows, wcols):
+def match_tiles(info, packed, tiles):
     smem = pl.BlockSpec(memory_space=pltpu.SMEM)
     vmem = pl.BlockSpec(memory_space=pltpu.VMEM)
-    hbm = pl.BlockSpec(memory_space=pl.ANY)
     return pl.pallas_call(
         match_kernel,
         out_shape=(
             jax.ShapeDtypeStruct((NCLASS * 32, SLOT, TILE), bf16),
             jax.ShapeDtypeStruct((NCLASS, 1, 128), i32),
         ),
-        in_specs=[smem, smem, hbm, vmem, vmem, hbm, hbm],
+        in_specs=[smem, vmem, pl.BlockSpec(memory_space=pl.ANY)],
         out_specs=(vmem, smem),
         scratch_shapes=[
             pltpu.VMEM((NTILE, TILE, TILE), bf16),
-            pltpu.VMEM((NTILE, BW * TILE), bf16),
-            pltpu.VMEM((NTILE, BW * TILE), bf16),
+            pltpu.VMEM((8, 128), f32),
+            pltpu.SMEM((8, 128), f32),
+            pltpu.VMEM((TILE, NBASIS * TILE), bf16),
+            pltpu.VMEM((NBASIS * TILE, TILE), bf16),
             pltpu.VMEM((NTILE, BW * TILE), f32),
             pltpu.VMEM((NTILE, BW * TILE), f32),
-            pltpu.VMEM((TILE, NBASIS * TILE), bf16),
-            pltpu.VMEM((NBASIS * TILE, TILE), bf16),
             pltpu.SMEM((NCLASS,), i32),
             pltpu.SMEM((NTILE,), i32),
-            pltpu.SemaphoreType.DMA((STEPS + 2,)),
+            pltpu.SemaphoreType.DMA((STEPS + 1,)),
         ],
-        compiler_params=pltpu.CompilerParams(vmem_limit_bytes=14 * MIB),
+        compiler_params=pltpu.CompilerParams(vmem_limit_bytes=24 * MIB),
         name="match",
-    )(info, coef, tiles, rtaps, ctaps, wrows, wcols)
+    )(info, packed, tiles)
 
 
 def greet(partners):
@@ -228,10 +216,10 @@
     top = jnp.max(loads[...], axis=0)
     n = 12
     for box, here, others in (
+        (box_z, z, column),
+        (box_b, band, [sibling]),
         (box_x, x, rings[:3]),
         (box_y, y, rings[3:]),
-        (box_z, z, column),
-        (box_b, band, [sibling]),
     ):
         box[here] = top
         shared = []
@@ -240,7 +228,7 @@
             n += 1
         for copy in shared:
             copy.start()
-        if box is box_y:
+        if box is box_z:
             for copy in large:
                 copy.start()
         for copy in shared:
@@ -279,7 +267,7 @@
     )(slots.reshape(NCLASS, 32, SLOT, TILE), meta)
 
 
-UNROLL = 4
+UNROLL = 8
 
 
 def warp_kernel(cap, meta, recv, slots, out, acc, fac, names, fill):
@@ -367,7 +355,7 @@
             pltpu.SMEM((NCLASS * 32,), i32),
             pltpu.SMEM((32,), i32),
         ],
-        compiler_params=pltpu.CompilerParams(vmem_limit_bytes=18 * MIB),
+        compiler_params=pltpu.CompilerParams(vmem_limit_bytes=36 * MIB),
         name="warp",
     )(meta, recv, slots)
 
@@ -530,11 +518,13 @@
 def body(
     tiles, psf_coeff, row_taps, col_taps, target_patch, offsets, visits, warp_rows, warp_cols, det_taps, band_weight
 ):
-    info = jnp.concatenate([target_patch[0, :, 0], offsets[0, :, 0], offsets[0, :, 1], visits[0]])
-    coef = psf_coeff[0].astype(f32).reshape(-1)
-    slots, meta = match_tiles(
-        info, coef, tiles[0].reshape(NTILE, TILE, TILE), row_taps, col_taps, warp_rows[0], warp_cols[0]
-    )
+    info = jnp.concatenate([target_patch[0].T, offsets[0].T, visits], axis=0)
+
+    def widened(lines):
+        return jnp.pad(lines, ((0, 16 - lines.shape[0]), (0, BW * TILE - lines.shape[1])))
+
+    packed = [warp_rows[0], warp_cols[0], widened(psf_coeff[0].T), widened(row_taps), widened(col_taps)]
+    slots, meta = match_tiles(info, jnp.concatenate(packed, axis=0), tiles[0].reshape(NTILE, TILE, TILE))
     recv, rmeta, most = route_tiles(slots, meta, CAP, 0)
 
     def few():

time: 137 us -> 125 us (0.912)
  Pallas kernels: 125 us -> 117 us
  local copies, waits for them, and re-layouts: 8.87 us -> 5.93 us
    pallas_call x1, Pallas kernels: 15.3 us -> 10.3 us  [match_tiles(): pl.pallas_call(match_kernel, out_shape=(jax.ShapeDtypeStruct((NCLASS * 32...]
    pallas_call x1, Pallas kernels: 14.8 us -> 11 us  [warp_tiles(): pl.pallas_call(functools.partial(warp_kernel, cap), out_shape=jax.ShapeDt...]
    unnamed x13 -> x21, local copies, waits for them, and re-layouts: 6.61 us -> 5.34 us
where the time goes in v3:
time: 125 us
  Pallas kernels  117 us (94%)
  local copies, waits for them, and re-layouts  5.93 us (5%)
  between operations  2.1 us (2%)
    pallas_call x1, Pallas kernels, merge(): pl.pallas_call(merge_kernel, out_shape=(image, image), in_specs=[vmem, sm...  54.2 us
    pallas_call x1, Pallas kernels, route_tiles(): pl.pallas_call(functools.partial(route_kernel, cap), out_shape=(jax.Shape...  41.1 us
    pallas_call x1, Pallas kernels, warp_tiles(): pl.pallas_call(functools.partial(warp_kernel, cap), out_shape=jax.ShapeDt...  11 us
    pallas_call x1, Pallas kernels, match_tiles(): pl.pallas_call(match_kernel, out_shape=(jax.ShapeDtypeStruct((NCLASS * 32...  10.3 us
    unnamed x21, local copies, waits for them, and re-layouts  5.34 us

profile of v3, /device:TPU:1, one launch (start us, length us, event | category | flops | bytes accessed | tf_op | source)
XLA Modules:
  0.0 124.7 jit_solution(4216167246076847419)
XLA Ops:
  0.6 0.0 copy-start.3
  0.6 0.0 copy-start.4
  0.7 0.0 copy-start.5
  0.7 0.0 copy-start.8
  0.7 0.0 copy-start.6
  0.7 0.0 copy-start.7
  0.7 2.2 %copy.13 = bf16[8,8,128,128]{3,2,1,0:T(8,128)(2,1)S(1)} copy(bf16[8,8,128,128]{3,1,2,0:T(8,128)(2,1)} %bitcast.26) | data formatting | bytes 4194304
  2.9 0.9 bitcast_dynamic-update-slice_fusion.1
  3.7 0.8 bitcast_dynamic-update-slice_fusion
  4.6 0.0 copy-done.3
  4.6 0.0 copy-done.4
  4.6 0.0 copy-done.5
  4.6 0.0 copy-done.8
  4.7 0.0 copy-done.6
  4.7 0.0 copy-done.7
  4.7 10.3 %match.1 = (bf16[256,144,128]{2,1,0:T(8,128)(2,1)S(1)}, s32[8,1,128]{2,1,0:T(1,128)S(1)}) custom-call(s32[4,64]{1,0:T(4,128)S(1)} %pad_add_fusion.info, bf16[176,512]{1,0:T(8,128)(2,1)S(1)} %pad_dynamic-update-slice_fusion.packed, bf16[64,128,128]{2,1,0:T(8,128)(2,1)S(1)} %bitcast.20), custom_call_target="tpu_custom_call" | custom-call | tf_op jit(solution)/shard_map/match/pallas_call | solution.py:132
  15.0 41.1 %route.3 = (bf16[8,16,144,128]{3,2,1,0:T(8,128)(2,1)S(1)}, s32[8,1,128]{2,1,0:T(1,128)S(1)}, s32[1,128]{1,0:T(1,128)S(1)}) custom-call(bf16[8,32,144,128]{3,2,1,0:T(8,128)(2,1)S(1)} %bitcast.22, s32[8,1,128]{2,1,0:T(1,128)S(1)} %get-tuple-element.31.meta), custom_call_target="tpu_custom_call" | custom-call | tf_op jit(solution)/shard_map/route/pallas_call | solution.py:244
  56.1 0.6 slice.3
  57.3 0.0 copy-start
  57.4 11.0 %conditional.1 = (bf16[2,4,4,272,256]{4,3,2,1,0:T(8,128)(2,1)}) conditional(s32[]{:T(128)} %bitcast.11, (s32[8,1,128]{2,1,0:T(1,128)S(1)}, bf16[8,16,144,128]{3,2,1,0:T(8,128)(2,1)S(1)}, bf16[256,144,128]{2,1,0:T(8,128)(2,1)S(1)}) %tuple.15, (bf16[256,144,128]{2,1,0:T(8,128)(2,1)S(1)}, s32[8,1,128]{2,1,0:T(1,128)S(1)}) %match.1), branch_computations={%region_0.1_spmd, %region_1.2_spmd} | conditional | bytes 75497536 | solution.py:537
  57.4 11.0 %warp.2 = bf16[32,272,256]{2,1,0:T(8,128)(2,1)} custom-call(s32[8,1,128]{2,1,0:T(1,128)S(1)} %get-tuple-element.14.meta, bf16[8,16,144,128]{3,2,1,0:T(8,128)(2,1)S(1)} %get-tuple-element.15.recv, bf16[256,144,128]{2,1,0:T(8,128)(2,1)S(1)} %get-tuple-element.16.slots), custom_call_target="tpu_custom_call" | custom-call | tf_op jit(solution)/shard_map/cond/branch_0_fun/warp/pallas_call | solution.py:347
  69.0 0.0 copy-done
  69.0 54.2 %merge.1 = (f32[256,256]{1,0:T(8,128)S(1)}, f32[256,256]{1,0:T(8,128)S(1)}) custom-call(bf16[2,4,4,272,256]{4,3,2,1,0:T(8,128)(2,1)} %get-tuple-element.41.part, f32[9]{0:T(128)S(1)} %copy-done, f32[1]{0:T(128)S(6)} %copy.22.weight), custom_call_target="tpu_custom_call" | custom-call | tf_op jit(solution)/shard_map/merge/pallas_call | solution.py:496
  123.3 0.7 copy.23
  124.0 0.7 copy.24
  (4 shorter events, 0.0 us)
Async XLA Ops:
  0.6 4.0 %copy-start.3 = (bf16[1,64,5]{1,2,0:T(8,128)(2,1)S(1)}, bf16[1,64,5]{1,2,0:T(8,128)(2,1)}, u32[]{:S(2)}) copy-start(bf16[1,64,5]{1,2,0:T(8,128)(2,1)} %param.14) | copy-start | bytes 1924
  0.6 4.0 %copy-start.4 = (bf16[5,41]{1,0:T(8,128)(2,1)S(1)}, bf16[5,41]{1,0:T(8,128)(2,1)}, u32[]{:S(2)}) copy-start(bf16[5,41]{1,0:T(8,128)(2,1)} %param.15) | copy-start | bytes 1234
  0.7 4.0 %copy-start.5 = (bf16[5,41]{1,0:T(8,128)(2,1)S(1)}, bf16[5,41]{1,0:T(8,128)(2,1)}, u32[]{:S(2)}) copy-start(bf16[5,41]{1,0:T(8,128)(2,1)} %param.16) | copy-start | bytes 1234
  0.7 4.0 %copy-start.8 = (s32[1,64,1]{1,2,0:T(1,128)S(1)}, s32[1,64,1]{1,2,0:T(1,128)}, u32[]{:S(2)}) copy-start(s32[1,64,1]{1,2,0:T(1,128)} %param.17) | copy-start | bytes 772
  0.7 4.0 %copy-start.6 = (s32[1,64,2]{1,2,0:T(2,128)S(1)}, s32[1,64,2]{1,2,0:T(2,128)}, u32[]{:S(2)}) copy-start(s32[1,64,2]{1,2,0:T(2,128)} %param.18) | copy-start | bytes 1540
  0.7 4.0 %copy-start.7 = (s32[1,64]{1,0:T(1,128)S(1)}, s32[1,64]{1,0:T(1,128)}, u32[]{:S(2)}) copy-start(s32[1,64]{1,0:T(1,128)} %param.19) | copy-start | bytes 772
  57.3 11.7 %copy-start = (f32[9]{0:T(128)S(1)}, f32[9]{0:T(128)}, u32[]{:S(2)}) copy-start(f32[9]{0:T(128)} %taps.1) | copy-start | bytes 112

commit v4 on v3

--- a/solution.py
+++ b/solution.py
@@ -196,30 +196,25 @@
     )
 
 
-def route_kernel(cap, slots, meta, recv, rmeta, most, loads, box_x, box_y, box_z, box_b, sends, recvs, local):
+def route_kernel(cap, slots, meta, recv, rmeta, most, box_p, box_z, box_b, sends, recvs, local):
     me, z, x, y = coords()
     band = lax.axis_index("band")
-    rings, column = ring_partners(), column_partners()
+    column = column_partners()
+    plane = [{"patch": z * 16 + lax.rem(me % 16 + d, 16)} for d in range(1, 16)]
     sibling = {"patch": me, "band": 1 - band}
-    greet(rings + column + [sibling])
+    greet(plane + column + [sibling])
     small = ring_copies(lambda a, i: meta.at[4 * a + i], lambda a, i: rmeta.at[4 * a + i], sends, recvs, 6)
     for n, own in enumerate((x, 4 + y)):
         small.append(pltpu.make_async_copy(meta.at[own], rmeta.at[own], local.at[n]))
     large = ring_copies(
         lambda a, i: slots.at[4 * a + i, pl.ds(0, cap)], lambda a, i: recv.at[4 * a + i], sends, recvs, 0
     )
-    fetch = pltpu.make_async_copy(meta, loads, local.at[2])
-    fetch.start()
-    for copy in small:
-        copy.start()
-    fetch.wait()
-    top = jnp.max(loads[...], axis=0)
+    top = jnp.max(meta[...], axis=0)
     n = 12
     for box, here, others in (
+        (box_p, me % 16, plane),
         (box_z, z, column),
         (box_b, band, [sibling]),
-        (box_x, x, rings[:3]),
-        (box_y, y, rings[3:]),
     ):
         box[here] = top
         shared = []
@@ -228,8 +223,8 @@
             n += 1
         for copy in shared:
             copy.start()
-        if box is box_z:
-            for copy in large:
+        if box is box_p:
+            for copy in small + large:
                 copy.start()
         for copy in shared:
             copy.wait()
@@ -248,17 +243,15 @@
             jax.ShapeDtypeStruct((NCLASS, 1, 128), i32),
             jax.ShapeDtypeStruct((1, 128), i32),
         ),
-        in_specs=[hbm, hbm],
+        in_specs=[hbm, pl.BlockSpec(memory_space=pltpu.VMEM)],
         out_specs=(hbm, hbm, pl.BlockSpec(memory_space=pltpu.VMEM)),
         scratch_shapes=[
-            pltpu.VMEM((NCLASS, 1, 128), i32),
-            pltpu.VMEM((4, 1, 128), i32),
-            pltpu.VMEM((4, 1, 128), i32),
+            pltpu.VMEM((16, 1, 128), i32),
             pltpu.VMEM((NZ, 1, 128), i32),
             pltpu.VMEM((2, 1, 128), i32),
-            pltpu.SemaphoreType.DMA((26,)),
-            pltpu.SemaphoreType.DMA((26,)),
-            pltpu.SemaphoreType.DMA((3,)),
+            pltpu.SemaphoreType.DMA((35,)),
+            pltpu.SemaphoreType.DMA((35,)),
+            pltpu.SemaphoreType.DMA((2,)),
         ],
         compiler_params=pltpu.CompilerParams(
             collective_id=collective_id, has_side_effects=True, vmem_limit_bytes=4 * MIB
@@ -288,13 +281,15 @@
     acc[...] = jnp.zeros_like(acc)
     fac[...] = jnp.zeros_like(fac)
     gap = lax.broadcasted_iota(i32, (PATCH, TILE), 0) - lax.broadcasted_iota(i32, (PATCH, TILE), 1)
+    gap = gap.astype(jnp.int16)
 
     def banded(lines, first, gaps, offset):
-        gaps = gaps - offset
-        mat = jnp.zeros(gaps.shape, f32)
+        gaps = gaps - offset.astype(jnp.int16)
+        mat = jnp.zeros(gaps.shape, bf16)
         for b in range(BW):
-            mat = jnp.where(gaps == b, lines[first + b : first + b + 1, :], mat)
-        return mat.astype(bf16)
+            line = lines[first + b : first + b + 1, :].astype(bf16)
+            mat = jnp.where(gaps == jnp.int16(b), line, mat)
+        return mat
 
     place = lax.broadcasted_iota(i32, (8, TILE), 0)
 
@@ -358,6 +353,16 @@
         compiler_params=pltpu.CompilerParams(vmem_limit_bytes=36 * MIB),
         name="warp",
     )(meta, recv, slots)
+
+
+def dot3(a, b):
+    a_high, b_high = a.astype(bf16), b.astype(bf16)
+    a_low, b_low = (a - a_high.astype(f32)).astype(bf16), (b - b_high.astype(f32)).astype(bf16)
+
+    def dot(p, q):
+        return jnp.dot(p, q, preferred_element_type=f32)
+
+    return dot(a_high, b_high) + (dot(a_low, b_high) + dot(a_high, b_low))
 
 
 def merge_kernel(
@@ -484,8 +489,8 @@
     top = jnp.where(me == 0, 0.0, halo[0, 0] + halo[0, 1])
     bottom = jnp.where(me == 127, 0.0, halo[1, 0] + halo[1, 1])
     padded = jnp.concatenate([top, mine[...] + other[...], bottom], axis=0)
-    row_pass = jnp.dot(rowk[...], padded, precision=lax.Precision.HIGHEST, preferred_element_type=f32)
-    detection[...] = jnp.dot(row_pass, colk[...], precision=lax.Precision.HIGHEST, preferred_element_type=f32)
+    row_pass = dot3(rowk[...], padded)
+    detection[...] = dot3(row_pass, colk[...])
 
 
 def merge(part, det_taps, band_weight):

time: 125 us -> 121 us (0.968)
  Pallas kernels: 117 us -> 113 us
    pallas_call x1, Pallas kernels: 41.1 us -> 38 us  [route_tiles(): pl.pallas_call(functools.partial(route_kernel, cap), out_shape=(jax.Shape...]
where the time goes in v4:
time: 121 us
  Pallas kernels  113 us (93%)
  local copies, waits for them, and re-layouts  5.93 us (5%)
  between operations  2.1 us (2%)
    pallas_call x1, Pallas kernels, merge(): pl.pallas_call(merge_kernel, out_shape=(image, image), in_specs=[vmem, sm...  53 us
    pallas_call x1, Pallas kernels, route_tiles(): pl.pallas_call(functools.partial(route_kernel, cap), out_shape=(jax.Shape...  38 us
    pallas_call x1, Pallas kernels, warp_tiles(): pl.pallas_call(functools.partial(warp_kernel, cap), out_shape=jax.ShapeDt...  11.6 us
    pallas_call x1, Pallas kernels, match_tiles(): pl.pallas_call(match_kernel, out_shape=(jax.ShapeDtypeStruct((NCLASS * 32...  10.3 us
    unnamed x21, local copies, waits for them, and re-layouts  5.34 us

profile of v4, /device:TPU:1, one launch (start us, length us, event | category | flops | bytes accessed | tf_op | source)
XLA Modules:
  0.0 121.0 jit_solution(7783629136572238116)
XLA Ops:
  0.6 0.0 copy-start.3
  0.6 0.0 copy-start.4
  0.7 0.0 copy-start.5
  0.7 0.0 copy-start.8
  0.7 0.0 copy-start.6
  0.7 0.0 copy-start.7
  0.7 2.2 %copy.13 = bf16[8,8,128,128]{3,2,1,0:T(8,128)(2,1)S(1)} copy(bf16[8,8,128,128]{3,1,2,0:T(8,128)(2,1)} %bitcast.26) | data formatting | bytes 4194304
  2.9 0.9 bitcast_dynamic-update-slice_fusion.1
  3.7 0.8 bitcast_dynamic-update-slice_fusion
  4.6 0.0 copy-done.3
  4.6 0.0 copy-done.4
  4.6 0.0 copy-done.5
  4.6 0.0 copy-done.8
  4.7 0.0 copy-done.6
  4.7 0.0 copy-done.7
  4.7 10.3 %match.1 = (bf16[256,144,128]{2,1,0:T(8,128)(2,1)S(1)}, s32[8,1,128]{2,1,0:T(1,128)S(1)}) custom-call(s32[4,64]{1,0:T(4,128)S(1)} %pad_add_fusion.info, bf16[176,512]{1,0:T(8,128)(2,1)S(1)} %pad_dynamic-update-slice_fusion.packed, bf16[64,128,128]{2,1,0:T(8,128)(2,1)S(1)} %bitcast.20), custom_call_target="tpu_custom_call" | custom-call | tf_op jit(solution)/shard_map/match/pallas_call | solution.py:132
  15.0 38.0 %route.3 = (bf16[8,16,144,128]{3,2,1,0:T(8,128)(2,1)S(1)}, s32[8,1,128]{2,1,0:T(1,128)S(1)}, s32[1,128]{1,0:T(1,128)S(1)}) custom-call(bf16[8,32,144,128]{3,2,1,0:T(8,128)(2,1)S(1)} %bitcast.22, s32[8,1,128]{2,1,0:T(1,128)S(1)} %get-tuple-element.31.meta), custom_call_target="tpu_custom_call" | custom-call | tf_op jit(solution)/shard_map/route/pallas_call | solution.py:239
  53.0 0.6 slice.3
  54.2 0.0 copy-start
  54.2 11.6 %conditional.1 = (bf16[2,4,4,272,256]{4,3,2,1,0:T(8,128)(2,1)}) conditional(s32[]{:T(128)} %bitcast.11, (s32[8,1,128]{2,1,0:T(1,128)S(1)}, bf16[8,16,144,128]{3,2,1,0:T(8,128)(2,1)S(1)}, bf16[256,144,128]{2,1,0:T(8,128)(2,1)S(1)}) %tuple.15, (bf16[256,144,128]{2,1,0:T(8,128)(2,1)S(1)}, s32[8,1,128]{2,1,0:T(1,128)S(1)}) %match.1), branch_computations={%region_0.1_spmd, %region_1.2_spmd} | conditional | bytes 75497536 | solution.py:542
  54.2 11.6 %warp.2 = bf16[32,272,256]{2,1,0:T(8,128)(2,1)} custom-call(s32[8,1,128]{2,1,0:T(1,128)S(1)} %get-tuple-element.14.meta, bf16[8,16,144,128]{3,2,1,0:T(8,128)(2,1)S(1)} %get-tuple-element.15.recv, bf16[256,144,128]{2,1,0:T(8,128)(2,1)S(1)} %get-tuple-element.16.slots), custom_call_target="tpu_custom_call" | custom-call | tf_op jit(solution)/shard_map/cond/branch_0_fun/warp/pallas_call | solution.py:342
  66.5 0.0 copy-done
  66.5 53.0 %merge.1 = (f32[256,256]{1,0:T(8,128)S(1)}, f32[256,256]{1,0:T(8,128)S(1)}) custom-call(bf16[2,4,4,272,256]{4,3,2,1,0:T(8,128)(2,1)} %get-tuple-element.41.part, f32[9]{0:T(128)S(1)} %copy-done, f32[1]{0:T(128)S(6)} %copy.22.weight), custom_call_target="tpu_custom_call" | custom-call | tf_op jit(solution)/shard_map/merge/pallas_call | solution.py:501
  119.5 0.7 copy.23
  120.3 0.7 copy.24
  (4 shorter events, 0.0 us)
Async XLA Ops:
  0.6 4.0 %copy-start.3 = (bf16[1,64,5]{1,2,0:T(8,128)(2,1)S(1)}, bf16[1,64,5]{1,2,0:T(8,128)(2,1)}, u32[]{:S(2)}) copy-start(bf16[1,64,5]{1,2,0:T(8,128)(2,1)} %param.14) | copy-start | bytes 1924
  0.6 4.0 %copy-start.4 = (bf16[5,41]{1,0:T(8,128)(2,1)S(1)}, bf16[5,41]{1,0:T(8,128)(2,1)}, u32[]{:S(2)}) copy-start(bf16[5,41]{1,0:T(8,128)(2,1)} %param.15) | copy-start | bytes 1234
  0.7 4.0 %copy-start.5 = (bf16[5,41]{1,0:T(8,128)(2,1)S(1)}, bf16[5,41]{1,0:T(8,128)(2,1)}, u32[]{:S(2)}) copy-start(bf16[5,41]{1,0:T(8,128)(2,1)} %param.16) | copy-start | bytes 1234
  0.7 4.0 %copy-start.8 = (s32[1,64,1]{1,2,0:T(1,128)S(1)}, s32[1,64,1]{1,2,0:T(1,128)}, u32[]{:S(2)}) copy-start(s32[1,64,1]{1,2,0:T(1,128)} %param.17) | copy-start | bytes 772
  0.7 4.0 %copy-start.6 = (s32[1,64,2]{1,2,0:T(2,128)S(1)}, s32[1,64,2]{1,2,0:T(2,128)}, u32[]{:S(2)}) copy-start(s32[1,64,2]{1,2,0:T(2,128)} %param.18) | copy-start | bytes 1540
  0.7 4.0 %copy-start.7 = (s32[1,64]{1,0:T(1,128)S(1)}, s32[1,64]{1,0:T(1,128)}, u32[]{:S(2)}) copy-start(s32[1,64]{1,0:T(1,128)} %param.19) | copy-start | bytes 772
  54.2 12.3 %copy-start = (f32[9]{0:T(128)S(1)}, f32[9]{0:T(128)}, u32[]{:S(2)}) copy-start(f32[9]{0:T(128)} %taps.1) | copy-start | bytes 112

commit v5 on v4

--- a/solution.py
+++ b/solution.py
@@ -170,7 +170,7 @@
 def ring_copies(send_block, recv_block, sends, recvs, first):
     me, z, x, y = coords()
     copies = []
-    for d in (2, 1, 3):
+    for d in (1, 3, 2):
         for axis, here in ((0, x), (1, y)):
             there = (here + d) % 4
             owner = z * 16 + there * 4 + y if axis == 0 else z * 16 + x * 4 + there
@@ -366,7 +366,7 @@
 
 
 def merge_kernel(
-    part, taps, weight, coadd, detection, recv, zpart, zrecv, mine, other, halo, rowk, colk, sends, recvs
+    part, taps, weight, coadd, detection, recv, zpart, zrecv, mine, other, halo, rowk, colk, aid, sends, recvs, aid_sends, aid_recvs
 ):
     me, z, x, y = coords()
     band = lax.axis_index("band")
@@ -405,7 +405,39 @@
     rowk[...] = row_kernel
     colk[...] = col_kernel
 
-    zcopies = []
+    zcopies, aids = [], []
+    half = CHUNK // 2
+
+    def z_copy(c, d, rows):
+        to = (z + d) % NZ
+        n = 6 * NCHUNK + 7 * c + d - 1
+        copy = remote(zpart.at[to, rows], zrecv.at[z, rows], sends.at[n], recvs.at[n], to * 16 + x * 4 + y)
+        copy.start()
+        return copy
+
+    def half_of(c, n):
+        return pl.ds(4 * FAC + c * CHUNK + n * half, half)
+
+    def aid_copy(c, n):
+        near_z = (z + (1 if n == 0 else NZ - 1)) % NZ
+        copy = remote(
+            zpart.at[(z + 4) % NZ, half_of(c, n)],
+            aid.at[c, n],
+            aid_sends.at[2 * c + n],
+            aid_recvs.at[2 * c + n],
+            near_z * 16 + x * 4 + y,
+        )
+        copy.start()
+        return copy
+
+    def send_far(c):
+        for n in range(2):
+            aids[c][n].wait()
+            d = 3 if n == 0 else 5
+            to, rows = (z + d) % NZ, half_of(c, n)
+            zpart[to, rows, :] = (zpart[to, rows, :].astype(f32) + aid[c, n].astype(f32)).astype(bf16)
+            zcopies[c].append(z_copy(c, d, rows_of(c, 4 * FAC)))
+
     for c in range(NCHUNK):
         for copy in pending[c]:
             copy.wait()
@@ -429,17 +461,13 @@
                 return carry
 
             lax.fori_loop(0, 4, fold, 0)
-        rows = rows_of(c, 4 * FAC)
-        copies = []
-        for d in (4, 3, 5, 2, 6, 1, 7):
-            to = (z + d) % NZ
-            n = 6 * NCHUNK + 7 * c + d - 1
-            copies.append(
-                remote(zpart.at[to, rows], zrecv.at[z, rows], sends.at[n], recvs.at[n], to * 16 + x * 4 + y)
-            )
-        for copy in copies:
-            copy.start()
-        zcopies.append(copies)
+        zcopies.append([z_copy(c, d, rows_of(c, 4 * FAC)) for d in (2, 6, 1, 7)])
+        if c == 0:
+            zcopies[c].append(z_copy(c, 4, pl.ds(0, 4 * FAC)))
+        aids.append([aid_copy(c, n) for n in range(2)])
+        if c:
+            send_far(c - 1)
+    send_far(NCHUNK - 1)
 
     cover = None
     last = []
@@ -463,7 +491,7 @@
             mine[...] = jnp.maximum(cover, 1.0)
         chunk = pl.ds(4 * FAC + c * CHUNK, CHUNK)
         total = zpart[z, chunk, :].astype(f32)
-        for d in range(1, NZ):
+        for d in (1, 2, 3, 5, 6, 7):
             total = total + zrecv[(z + d) % NZ, chunk, :].astype(f32)
         rows = slice(c * CHUNK, (c + 1) * CHUNK)
         image = total / mine[rows, :]
@@ -512,8 +540,11 @@
             pltpu.VMEM((2, 2, 8, PATCH), f32),
             pltpu.VMEM((PATCH, PATCH + 16), f32),
             pltpu.VMEM((PATCH, PATCH), f32),
+            pltpu.VMEM((NCHUNK, 2, CHUNK // 2, PATCH), bf16),
             pltpu.SemaphoreType.DMA((count,)),
             pltpu.SemaphoreType.DMA((count,)),
+            pltpu.SemaphoreType.DMA((2 * NCHUNK,)),
+            pltpu.SemaphoreType.DMA((2 * NCHUNK,)),
         ],
         compiler_params=pltpu.CompilerParams(collective_id=2, has_side_effects=True, vmem_limit_bytes=14 * MIB),
         name="merge",

time: 121 us -> 122 us (level)
    pallas_call x1, Pallas kernels: 53 us -> 54.3 us  [merge(): pl.pallas_call(merge_kernel, out_shape=(image, image), in_specs=[vmem, sm...]
where the time goes in v5:
time: 122 us
  Pallas kernels  113 us (93%)
  local copies, waits for them, and re-layouts  5.93 us (5%)
  between operations  2.1 us (2%)
    pallas_call x1, Pallas kernels, merge(): pl.pallas_call(merge_kernel, out_shape=(image, image), in_specs=[vmem, sm...  54.3 us
    pallas_call x1, Pallas kernels, route_tiles(): pl.pallas_call(functools.partial(route_kernel, cap), out_shape=(jax.Shape...  37.3 us
    pallas_call x1, Pallas kernels, warp_tiles(): pl.pallas_call(functools.partial(warp_kernel, cap), out_shape=jax.ShapeDt...  11.6 us
    pallas_call x1, Pallas kernels, match_tiles(): pl.pallas_call(match_kernel, out_shape=(jax.ShapeDtypeStruct((NCLASS * 32...  10.3 us
    unnamed x21, local copies, waits for them, and re-layouts  5.34 us

profile of v5, /device:TPU:1, one launch (start us, length us, event | category | flops | bytes accessed | tf_op | source)
XLA Modules:
  0.0 121.5 jit_solution(18217018321477193317)
XLA Ops:
  0.6 0.0 copy-start.3
  0.6 0.0 copy-start.4
  0.7 0.0 copy-start.5
  0.7 0.0 copy-start.8
  0.7 0.0 copy-start.6
  0.7 0.0 copy-start.7
  0.7 2.2 %copy.13 = bf16[8,8,128,128]{3,2,1,0:T(8,128)(2,1)S(1)} copy(bf16[8,8,128,128]{3,1,2,0:T(8,128)(2,1)} %bitcast.26) | data formatting | bytes 4194304
  2.9 0.9 bitcast_dynamic-update-slice_fusion.1
  3.7 0.8 bitcast_dynamic-update-slice_fusion
  4.6 0.0 copy-done.3
  4.6 0.0 copy-done.4
  4.6 0.0 copy-done.5
  4.6 0.0 copy-done.8
  4.7 0.0 copy-done.6
  4.7 0.0 copy-done.7
  4.7 10.3 %match.1 = (bf16[256,144,128]{2,1,0:T(8,128)(2,1)S(1)}, s32[8,1,128]{2,1,0:T(1,128)S(1)}) custom-call(s32[4,64]{1,0:T(4,128)S(1)} %pad_add_fusion.info, bf16[176,512]{1,0:T(8,128)(2,1)S(1)} %pad_dynamic-update-slice_fusion.packed, bf16[64,128,128]{2,1,0:T(8,128)(2,1)S(1)} %bitcast.20), custom_call_target="tpu_custom_call" | custom-call | tf_op jit(solution)/shard_map/match/pallas_call | solution.py:132
  15.0 37.3 %route.3 = (bf16[8,16,144,128]{3,2,1,0:T(8,128)(2,1)S(1)}, s32[8,1,128]{2,1,0:T(1,128)S(1)}, s32[1,128]{1,0:T(1,128)S(1)}) custom-call(bf16[8,32,144,128]{3,2,1,0:T(8,128)(2,1)S(1)} %bitcast.22, s32[8,1,128]{2,1,0:T(1,128)S(1)} %get-tuple-element.31.meta), custom_call_target="tpu_custom_call" | custom-call | tf_op jit(solution)/shard_map/route/pallas_call | solution.py:239
  52.3 0.6 slice.3
  53.5 0.0 copy-start
  53.5 11.6 %conditional.1 = (bf16[2,4,4,272,256]{4,3,2,1,0:T(8,128)(2,1)}) conditional(s32[]{:T(128)} %bitcast.11, (s32[8,1,128]{2,1,0:T(1,128)S(1)}, bf16[8,16,144,128]{3,2,1,0:T(8,128)(2,1)S(1)}, bf16[256,144,128]{2,1,0:T(8,128)(2,1)S(1)}) %tuple.15, (bf16[256,144,128]{2,1,0:T(8,128)(2,1)S(1)}, s32[8,1,128]{2,1,0:T(1,128)S(1)}) %match.1), branch_computations={%region_0.1_spmd, %region_1.2_spmd} | conditional | bytes 75497536 | solution.py:573
  53.5 11.6 %warp.2 = bf16[32,272,256]{2,1,0:T(8,128)(2,1)} custom-call(s32[8,1,128]{2,1,0:T(1,128)S(1)} %get-tuple-element.14.meta, bf16[8,16,144,128]{3,2,1,0:T(8,128)(2,1)S(1)} %get-tuple-element.15.recv, bf16[256,144,128]{2,1,0:T(8,128)(2,1)S(1)} %get-tuple-element.16.slots), custom_call_target="tpu_custom_call" | custom-call | tf_op jit(solution)/shard_map/cond/branch_0_fun/warp/pallas_call | solution.py:342
  65.8 0.0 copy-done
  65.8 54.3 %merge.1 = (f32[256,256]{1,0:T(8,128)S(1)}, f32[256,256]{1,0:T(8,128)S(1)}) custom-call(bf16[2,4,4,272,256]{4,3,2,1,0:T(8,128)(2,1)} %get-tuple-element.41.part, f32[9]{0:T(128)S(1)} %copy-done, f32[1]{0:T(128)S(6)} %copy.22.weight), custom_call_target="tpu_custom_call" | custom-call | tf_op jit(solution)/shard_map/merge/pallas_call | solution.py:529
  120.1 0.7 copy.23
  120.8 0.7 copy.24
  (4 shorter events, 0.0 us)
Async XLA Ops:
  0.6 4.0 %copy-start.3 = (bf16[1,64,5]{1,2,0:T(8,128)(2,1)S(1)}, bf16[1,64,5]{1,2,0:T(8,128)(2,1)}, u32[]{:S(2)}) copy-start(bf16[1,64,5]{1,2,0:T(8,128)(2,1)} %param.14) | copy-start | bytes 1924
  0.6 4.0 %copy-start.4 = (bf16[5,41]{1,0:T(8,128)(2,1)S(1)}, bf16[5,41]{1,0:T(8,128)(2,1)}, u32[]{:S(2)}) copy-start(bf16[5,41]{1,0:T(8,128)(2,1)} %param.15) | copy-start | bytes 1234
  0.7 4.0 %copy-start.5 = (bf16[5,41]{1,0:T(8,128)(2,1)S(1)}, bf16[5,41]{1,0:T(8,128)(2,1)}, u32[]{:S(2)}) copy-start(bf16[5,41]{1,0:T(8,128)(2,1)} %param.16) | copy-start | bytes 1234
  0.7 4.0 %copy-start.8 = (s32[1,64,1]{1,2,0:T(1,128)S(1)}, s32[1,64,1]{1,2,0:T(1,128)}, u32[]{:S(2)}) copy-start(s32[1,64,1]{1,2,0:T(1,128)} %param.17) | copy-start | bytes 772
  0.7 4.0 %copy-start.6 = (s32[1,64,2]{1,2,0:T(2,128)S(1)}, s32[1,64,2]{1,2,0:T(2,128)}, u32[]{:S(2)}) copy-start(s32[1,64,2]{1,2,0:T(2,128)} %param.18) | copy-start | bytes 1540
  0.7 4.0 %copy-start.7 = (s32[1,64]{1,0:T(1,128)S(1)}, s32[1,64]{1,0:T(1,128)}, u32[]{:S(2)}) copy-start(s32[1,64]{1,0:T(1,128)} %param.19) | copy-start | bytes 772
  53.5 12.3 %copy-start = (f32[9]{0:T(128)S(1)}, f32[9]{0:T(128)}, u32[]{:S(2)}) copy-start(f32[9]{0:T(128)} %taps.1) | copy-start | bytes 112
